TPU v7x, 128 devices: a whole 4x4x4 slice. The times are simulated.
128 devices in a mesh: grp: 4 (over y), col: 32 (over x, z, core).
Axes of the slice: x: 4, y: 4, z: 4, core: 2. Of those that a mesh axis runs over, the one named last changes fastest.
Arguments:
- tile_entries: bfloat16 [9216, 256, 256], P(('grp', 'col')), may hold values from -0.03125 to 0.03125
- slot_tile_row: int32 [9216], P(('grp', 'col')), may hold values from 0 to 15, as said below
- slot_tile_column: int32 [9216], P(('grp', 'col')), may hold values from 0 to 15
- tile_count: int32 [128], P(('grp', 'col')), may hold values from 24 to 72, as said below
- test_matrix: bfloat16 [131072, 320], P('col'), may hold values from -6 to 6
Outputs:
- basis: float32 [16384, 320], P(('grp', 'col'))
- projected: float32 [131072, 320], P('col')
Inputs may be any that keep to these rules, and one draw needn't show every extreme that they name: Slots at or past a device's tile_count are not part of the matrix. The live slots of one device hold distinct (slot_tile_row, slot_tile_column) pairs. `tile_count`: some device has all 72 slots live.
All inputs are finite; a program needn't handle non-finite values.
Results may differ from a plain program's by a relative error of at most 0.0027.
Values may be sent and summed in bfloat16 or wider, within the bound.
A program may use at most 128 MiB of HBM per device.

v0:
```python
import jax
import jax.numpy as jnp
from jax import lax
from jax.sharding import PartitionSpec as P

GROUP_TILE_ROWS = 16
SHARD_TILE_COLS = 16


def padded_terms(tile_entries, pick_idx, place_idx, active_count, operand, out_blocks, einsum_form):
    edge_len = tile_entries.shape[1]
    width = operand.shape[1]
    gathered = operand.reshape(-1, edge_len, width)[pick_idx]
    products = jnp.einsum(einsum_form, tile_entries, gathered, preferred_element_type=jnp.float32)
    live_mask = (jnp.arange(pick_idx.shape[0]) < active_count).astype(jnp.float32)
    empty = jnp.zeros((out_blocks, edge_len, width), jnp.float32)
    summed = empty.at[place_idx].add(products * live_mask[:, None, None])
    return summed.reshape(out_blocks * edge_len, width)


def orthonormal(sample, gram):
    lower = jnp.linalg.cholesky(gram)
    return jax.scipy.linalg.solve_triangular(lower, sample.T, lower=True).T


def local(tile_entries, slot_tile_row, slot_tile_column, tile_count, test_matrix):
    edge_len = tile_entries.shape[1]
    active_count = tile_count[0]
    grp_devices = lax.axis_size("grp")
    row_len = GROUP_TILE_ROWS * edge_len
    total_rows = row_len * grp_devices
    partial_sample = padded_terms(
        tile_entries,
        slot_tile_column,
        slot_tile_row,
        active_count,
        test_matrix,
        GROUP_TILE_ROWS,
        "tij,tjk->tik",
    )
    sample_share = lax.psum_scatter(partial_sample, "col", scatter_dimension=0, tiled=True)
    local_gram = jnp.dot(sample_share.T, sample_share, precision=lax.Precision.HIGHEST)
    gram = lax.psum(local_gram, ("grp", "col")) / total_rows
    basis = orthonormal(sample_share, gram)
    half_of_group = lax.all_gather(basis.astype(jnp.bfloat16), "col", axis=0, tiled=True)
    partial_proj = padded_terms(
        tile_entries,
        slot_tile_row,
        slot_tile_column,
        active_count,
        half_of_group,
        SHARD_TILE_COLS,
        "azh,azm->ahm",
    )
    projected = lax.psum(partial_proj, "grp")
    return (basis, projected)


def solution(mesh):
    placed = (
        P(("grp", "col"), None, None),
        P(("grp", "col")),
        P(("grp", "col")),
        P(("grp", "col")),
        P("col", None),
    )
    return jax.shard_map(
        local,
        mesh=mesh,
        in_specs=placed,
        out_specs=(P(("grp", "col"), None), P("col", None)),
        check_vma=False,
    )
```

profile of v0, /device:TPU:0, one launch (start us, length us, event | category | flops | bytes accessed | tf_op | source)
XLA Modules:
  0.0 665.8 jit_solution(5719303332809325945)
XLA Ops:
  7.2 0.7 compare_select_fusion
  7.9 2.0 copy.28
  10.5 0.7 compare_select_fusion.1
  11.2 6.8 %gather_fusion = bf16[72,256,320]{1,2,0:T(8,128)(2,1)} fusion(bf16[16,256,320]{1,2,0:T(8,128)(2,1)S(1)} %bitcast.71, s32[1024]{0:T(1024)S(1)} %pad_clamp_fusion.1), kind=kCustom, calls=%fused_computation | custom fusion | bytes 23593248 | tf_op jit(solution)/shard_map/gather | solution.py:13
  18.0 13.8 %multiply_bitcast_fusion.1 = f32[72,256,320]{1,2,0:T(8,128)} fusion(f32[72]{0:T(128)S(1)} %compare_convert_fusion, bf16[72,256,320]{1,2,0:T(8,128)(2,1)} %gather_fusion, bf16[72,256,256]{2,1,0:T(8,128)(2,1)} %param.5), kind=kOutput, calls=%fused_computation.7 | convolution fusion | flops 3025797120 | bytes 44826912 | tf_op jit(solution)/shard_map/tij,tjk->tik/dot_general | solution.py:14
  31.8 2.9 broadcast.172.clone
  34.7 46.9 %scatter_fusion = f32[16,256,320]{1,2,0:T(8,128)} fusion(f32[16,256,320]{1,2,0:T(8,128)} %broadcast.172.clone, s32[72]{0:T(128)S(1)} %compare_select_fusion.1, f32[72,256,320]{1,2,0:T(8,128)} %multiply_bitcast_fusion.1), kind=kCustom, calls=%fused_computation.2 | custom fusion | flops 5898240 | bytes 70779168 | tf_op jit(solution)/shard_map/scatter-add | solution.py:17
  81.6 5.5 copy.23
  87.2 87.2 %reduce-scatter.2.cloned.1.call-done = f32[128,320]{0,1:T(8,128)} async-done(((f32[4096,320]{0,1:T(8,128)}), f32[128,320]{0,1:T(8,128)}) %reduce-scatter.2.cloned.1.call-update) | async-done | bytes 163856 | tf_op jit(solution)/shard_map/reduce_scatter | solution.py:41
  174.4 2.3 fusion.21
  176.7 0.2 all-gather.2.cloned.1.call-start
  177.0 146.6 %all-reduce.6.cloned.1.call-done = f32[320,320]{0,1:T(8,128)} async-done(((f32[320,320]{0,1:T(8,128)}), f32[320,320]{0,1:T(8,128)}) %all-reduce.6.cloned.1.call-update) | async-done | bytes 409616 | tf_op jit(solution)/shard_map/psum | solution.py:43
  323.6 1.1 broadcast_multiply_fusion
  324.6 0.2 copy.17
  324.9 1.1 fusion
  326.0 11.7 %cholesky.78 = f32[128,128]{1,0:T(8,128)S(1)} custom-call(f32[128,128]{1,0:T(8,128)S(1)} %cholesky.198), custom_call_target="Cholesky" | custom-call | tf_op jit(solution)/shard_map/jit(cholesky)/cholesky | solution.py:22
  337.7 9.8 %custom-call.23 = f32[1,128,128]{1,2,0:T(8,128)S(1)} custom-call(f32[1,128,128]{2,1,0:T(8,128)S(1)} %get-tuple-element.26), custom_call_target="InvertDiagBlocksLowerTriangular" | custom-call | tf_op jit(solution)/shard_map/jit(cholesky)/cholesky | solution.py:22
  347.6 0.2 constant_dynamic-update-slice_fusion.2
  347.8 0.3 convolution_subtract_fusion
  348.1 11.7 %cholesky.164 = f32[128,128]{1,0:T(8,128)S(1)} custom-call(f32[128,128]{1,0:T(8,128)S(1)} %cholesky.202), custom_call_target="Cholesky" | custom-call | tf_op jit(solution)/shard_map/jit(cholesky)/cholesky | solution.py:22
  359.9 10.0 %custom-call.24 = f32[1,128,128]{1,2,0:T(8,128)S(1)} custom-call(f32[1,128,128]{2,1,0:T(8,128)S(1)} %get-tuple-element.23), custom_call_target="InvertDiagBlocksLowerTriangular" | custom-call | tf_op jit(solution)/shard_map/jit(cholesky)/cholesky | solution.py:22
  369.9 0.2 convolution_dynamic-update-slice_fusion
  370.1 0.2 convolution_subtract_fusion.3
  370.3 5.8 cholesky.186
  376.1 0.7 compare_reduce_fusion
  376.9 0.6 compare_reduce_fusion.1
  379.6 4.0 while.1
  379.6 0.6 fusion.33
  380.2 1.4 bitcast_dynamic-update-slice_fusion.2
  381.6 0.6 fusion.33
  382.2 1.4 bitcast_dynamic-update-slice_fusion.2
  383.6 0.1 fusion.11
  383.7 29.5 %custom-call.25 = f32[3,128,128]{1,2,0:T(8,128)S(1)} custom-call(f32[3,128,128]{2,1,0:T(8,128)S(1)} %pad_maximum_fusion), custom_call_target="InvertDiagBlocksLowerTriangular" | custom-call | tf_op jit(solution)/shard_map/jit(_solve_triangular)/triangular_solve | solution.py:23
  413.2 1.1 fusion.9
  414.4 1.0 convolution_subtract_fusion.1
  415.4 0.3 fusion.8
  415.7 1.0 convolution_subtract_fusion.2
  416.7 0.2 fusion.16
  416.9 0.7 fusion.19
  417.7 44.8 %all-gather.2.cloned.1.call-done = bf16[4096,320]{0,1:T(8,128)(2,1)} async-done(((bf16[128,320]{0,1:T(8,128)(2,1)}), bf16[4096,320]{0,1:T(8,128)(2,1)}) %all-gather.2.cloned.1.call-update) | async-done | bytes 2621456 | tf_op jit(solution)/shard_map/all_gather | solution.py:45
  462.5 2.0 copy.27
  464.5 6.8 %gather_fusion.1 = bf16[72,256,320]{1,2,0:T(8,128)(2,1)} fusion(bf16[16,256,320]{1,2,0:T(8,128)(2,1)S(1)} %bitcast.72, s32[1024]{0:T(1024)S(1)} %pad_clamp_fusion), kind=kCustom, calls=%fused_computation.1 | custom fusion | bytes 23593248 | tf_op jit(solution)/shard_map/gather | solution.py:13
  471.3 18.1 %multiply_bitcast_fusion = f32[72,256,320]{1,2,0:T(8,128)} fusion(f32[72]{0:T(128)S(1)} %compare_convert_fusion, bf16[72,256,320]{1,2,0:T(8,128)(2,1)} %gather_fusion.1, bf16[72,256,256]{2,1,0:T(8,128)(2,1)} %param.5), kind=kOutput, calls=%fused_computation.6 | convolution fusion | flops 3025797120 | bytes 44826912 | tf_op jit(solution)/shard_map/azh,azm->ahm/dot_general | solution.py:14
  489.4 2.9 broadcast.172
  492.3 46.2 %scatter_fusion.1 = f32[16,256,320]{1,2,0:T(8,128)} fusion(f32[16,256,320]{1,2,0:T(8,128)} %broadcast.172, s32[72]{0:T(128)S(1)} %compare_select_fusion, f32[72,256,320]{1,2,0:T(8,128)} %multiply_bitcast_fusion), kind=kCustom, calls=%fused_computation.3 | custom fusion | flops 5898240 | bytes 70779168 | tf_op jit(solution)/shard_map/scatter-add | solution.py:17
  538.5 5.6 copy.24
  544.1 109.8 %all-reduce.8.cloned.1.call-done = f32[4096,320]{0,1:T(8,128)} async-done(((f32[4096,320]{0,1:T(8,128)}), f32[4096,320]{0,1:T(8,128)}) %all-reduce.8.cloned.1.call-update) | async-done | bytes 5242896 | tf_op jit(solution)/shard_map/psum | solution.py:55
  653.9 5.4 copy.48
  (26 shorter events, 0.5 us)
Async XLA Ops:
  7.2 167.2 %reduce-scatter.2.cloned.1.call-start = ((), (), s32[]{:S(2)}) async-start(), calls=%async_computation.1 | async-start | bytes 5406720 | tf_op jit(solution)/shard_map/reduce_scatter | solution.py:41
  87.1 236.4 %all-reduce.6.cloned.1.call-start = ((), (), s32[]{:S(2)}) async-start(), calls=%async_computation.2 | async-start | bytes 983040 | tf_op jit(solution)/shard_map/psum | solution.py:43
  176.7 285.8 %all-gather.2.cloned.1.call-start = ((), (), s32[]{:S(2)}) async-start(), calls=%async_computation.3 | async-start | bytes 2703360 | tf_op jit(solution)/shard_map/all_gather | solution.py:45
  417.7 236.2 %all-reduce.8.cloned.1.call-start = ((), (), s32[]{:S(2)}) async-start(), calls=%async_computation.4 | async-start | bytes 10485760 | tf_op jit(solution)/shard_map/psum | solution.py:55
Sparse Core Ops, SparseCore 0:
  87.3 87.0 reduce-scatter.1
  180.4 143.0 all-reduce.5
  417.8 44.7 all-gather.1
  544.2 109.6 all-reduce.7
where the time goes:
time: 667 us; the launch traced here: 666 us
  waiting for transfers between devices  388 us (58%)
  other arithmetic  177 us (27%)
  local copies, waits for them, and re-layouts  44.2 us (7%)
  matrix products  38.7 us (6%)
  between operations  16.6 us (2%)
    psum x1, waiting for transfers between devices, local(): gram = lax.psum(local_gram, ('grp', 'col')) / total_rows  147 us
    psum x1, waiting for transfers between devices, local(): projected = lax.psum(partial_proj, 'grp')  110 us
    scatter-add x2, other arithmetic, padded_terms(): summed = empty.at[place_idx].add(products * live_mask[:, None, None])  93.1 us
    reduce_scatter x1, waiting for transfers between devices, local(): lax.psum_scatter(partial_sample, 'col', scatter_dimension=0, tiled=True)  87.2 us
    another operation x10, other arithmetic, orthonormal(): lower = jnp.linalg.cholesky(gram)  50.5 us
    all_gather x1, waiting for transfers between devices, local(): lax.all_gather(basis.astype(jnp.bfloat16), 'col', axis=0, tiled=True)  44.8 us
    dot_general x2, matrix products, padded_terms(): jnp.einsum(einsum_form, tile_entries, gathered, preferred_element_type=jn...  31.8 us
    another operation x7, other arithmetic, orthonormal(): return jax.scipy.linalg.solve_triangular(lower, sample.T, lower=True).T  29.7 us
  transfers between devices with their start and end apart: 4, of which 4 were waited for; matrix products, arithmetic and copies ran while one was open for 0% of the time, Pallas kernels for 0%

commit v1 on v0

v1 whole, which is shorter than its diff:
```python
import functools

import jax
import jax.numpy as jnp
from jax import lax
from jax.experimental import pallas as pl
from jax.experimental.pallas import tpu as pltpu
from jax.sharding import PartitionSpec as P

MESH = pl.DeviceIdType.MESH
EDGE = 256
K = 320
HALF = 160
PART = 80
SLOTS = 72
GROUP = 8
NB = 16
BLK = 64
ROWS = 16384
F32 = jnp.float32
BF16 = jnp.bfloat16
I16 = jnp.int16
VMEM_LIMIT = 60 * 1024 * 1024
HIGHEST = lax.Precision.HIGHEST


def nn(a, b, **kw):
    return lax.dot_general(a, b, (((1,), (0,)), ((), ())), preferred_element_type=F32, **kw)


def nt(a, b, **kw):
    return lax.dot_general(a, b, (((1,), (1,)), ((), ())), preferred_element_type=F32, **kw)


def tn(a, b, **kw):
    return lax.dot_general(a, b, (((0,), (0,)), ((), ())), preferred_element_type=F32, **kw)


def scale_of(peak):
    top = jnp.maximum(jnp.max(peak, axis=1, keepdims=True), 1e-30)
    return top * (1.0 / 32767.0), 32767.0 / top


def encode(value, inverse):
    return jnp.round(value * inverse).astype(jnp.int32).astype(I16)


def decode(code, scale):
    return code.astype(jnp.int32).astype(F32) * scale


def pack(scale, first=0):
    lane = lax.broadcasted_iota(jnp.int32, (8, 128), 1)
    packed = jnp.zeros((8, 128), F32)
    for m in range(scale.shape[0] // 8):
        packed = jnp.where(lane == first + m, scale[8 * m : 8 * m + 8], packed)
    return packed


def unpack(packed, first, rows):
    return jnp.concatenate([packed[:, first + m : first + m + 1] for m in range(rows // 8)], axis=0)


def split(value):
    high = value.astype(BF16)
    return high, (value - high.astype(F32)).astype(BF16)


def finish_codes(acc, store, packed_ref):
    def peak_step(i, peak):
        block = jnp.abs(acc[i])
        return jnp.maximum(peak, jnp.maximum(block[:, :128], block[:, 128:]))

    peak = lax.fori_loop(0, NB, peak_step, jnp.zeros((K, 128), F32))
    scale, inverse = scale_of(peak)
    packed_ref[...] = pack(scale)

    def code_step(i, carry):
        store(i, encode(acc[i], inverse))
        return carry

    lax.fori_loop(0, NB, code_step, 0)


def sample_kernel(row_s, col_s, count_s, tiles, omega, codes, packed, omega_t, acc):
    step = pl.program_id(0)

    @pl.when(step == 0)
    def _():
        def flip(i, carry):
            omega_t[i] = omega[pl.ds(pl.multiple_of(i * EDGE, EDGE), EDGE), :].T
            acc[i] = jnp.zeros((K, EDGE), F32)
            return carry

        lax.fori_loop(0, NB, flip, 0)

    for u in range(GROUP):
        slot = step * GROUP + u
        row = jnp.where(slot < count_s[0], row_s[slot], NB)
        acc[row] += nt(omega_t[col_s[slot]], tiles[u])

    @pl.when(step == SLOTS // GROUP - 1)
    def _():
        def store(i, code):
            codes[i, 0] = code[:, :128]
            codes[i, 1] = code[:, 128:]

        finish_codes(acc, store, packed)


def project_kernel(row_s, col_s, count_s, tiles, s_codes, s_packed, codes, packed, s_split, acc):
    step = pl.program_id(0)

    @pl.when(step == 0)
    def _():
        def widen(i, carry):
            for core in range(2):
                high, low = split(decode(s_codes[i, core], unpack(s_packed[i, core], 0, K)))
                s_split[i, :K, core * 128 : core * 128 + 128] = high
                s_split[i, K:, core * 128 : core * 128 + 128] = low
            acc[i] = jnp.zeros((K, EDGE), F32)
            return carry

        lax.fori_loop(0, NB, widen, 0)

    for u in range(GROUP):
        slot = step * GROUP + u
        col = jnp.where(slot < count_s[0], col_s[slot], NB)
        both = nn(s_split[row_s[slot]], tiles[u])
        acc[col] += both[:K] + both[K:]

    @pl.when(step == SLOTS // GROUP - 1)
    def _():
        def store(i, code):
            codes[i] = code

        finish_codes(acc, store, packed)


def xor2(a, b):
    return (a % 2 + b % 2) % 2 + 2 * ((a // 2 + b // 2) % 2)


GENERATORS = (4, 12, 1, 3)


def span(generators):
    out = [0]
    for g in generators:
        out = out + [w ^ g for w in out]
    return out


def order_of(part):
    return GENERATORS[part:] + GENERATORS[:part]


def plane_kernel(
    codes, packed, share, out_codes, out_packed,
    pair_codes, pair_packed, total, *rest,
):
    sends, recvs = rest[0:4], rest[4:8]
    (
        send_packed, recv_packed, sem_pair, sem_rs_s, sem_rs_r, sem_rsp_s, sem_rsp_r,
        sem_ag_s, sem_ag_r, sem_agp_s, sem_agp_r, sem_fw_s, sem_fw_r, sem_fwp_s, sem_fwp_r,
    ) = rest[8:]
    me = lax.axis_index("col")
    chip, core = me // 2, me % 2
    x, z = chip // 4, chip % 4
    other = 1 - core

    def chip_at(w):
        return xor2(x, w // 4) * 4 + xor2(z, w % 4)

    sibling = chip * 2 + other
    peers = {g: chip_at(g) * 2 + core for g in GENERATORS}

    barrier = pltpu.get_barrier_semaphore()
    for peer in [sibling] + list(peers.values()):
        pl.semaphore_signal(barrier, inc=1, device_id={"col": peer}, device_id_type=MESH)
    pl.semaphore_wait(barrier, 5)

    def remote(src, dst, s, r, peer):
        copy = pltpu.make_async_remote_copy(
            src_ref=src, dst_ref=dst, send_sem=s, recv_sem=r,
            device_id={"col": peer}, device_id_type=MESH,
        )
        copy.start()
        return copy

    first = remote(codes.at[:, other], pair_codes, sem_pair.at[0], sem_pair.at[1], sibling)
    first_packed = remote(packed, pair_packed, sem_pair.at[2], sem_pair.at[3], sibling)
    own_scale = unpack(packed[...], 0, K)
    first_packed.wait()
    pair_scale = unpack(pair_packed[...], 0, K)
    first.wait()

    def join(w, carry):
        i = chip_at(w)
        total[w] = decode(codes[i, core], own_scale) + decode(pair_codes[i], pair_scale)
        return carry

    lax.fori_loop(0, NB, join, 0)

    started = {}

    def rs_send(part, t):
        gens = order_of(part)
        rows = slice(part * PART, part * PART + PART)
        blocks = [gens[t] ^ w for w in span(gens[t + 1 :])]
        peak = jnp.abs(total[blocks[0], rows])
        for w in blocks[1:]:
            peak = jnp.maximum(peak, jnp.abs(total[w, rows]))
        scale, inverse = scale_of(peak)
        send_packed[part, t] = pack(scale)
        for n, w in enumerate(blocks):
            sends[t][part, n] = encode(total[w, rows], inverse)
        started[part, t] = (
            remote(sends[t].at[part], recvs[t].at[part], sem_rs_s.at[part, t], sem_rs_r.at[part, t], peers[gens[t]]),
            remote(send_packed.at[part, t], recv_packed.at[part, t], sem_rsp_s.at[part, t], sem_rsp_r.at[part, t], peers[gens[t]]),
        )

    def rs_take(part, t):
        gens = order_of(part)
        rows = slice(part * PART, part * PART + PART)
        for copy in started[part, t]:
            copy.wait()
        scale = unpack(recv_packed[part, t], 0, PART)
        for n, w in enumerate(span(gens[t + 1 :])):
            total[w, rows] += decode(recvs[t][part, n], scale)

    for t in range(4):
        for part in range(4):
            if t > 0:
                rs_take(part, t - 1)
            rs_send(part, t)
    for part in range(4):
        rs_take(part, 3)

    mine = total[0]
    share[...] = mine
    scale, inverse = scale_of(jnp.abs(mine))
    out_codes[chip, core] = encode(mine, inverse)
    out_packed[chip, core] = pack(scale)

    pending = []

    def to_sibling(part, w):
        i = chip_at(w)
        rows = pl.ds(part * PART, PART)
        ref = out_codes.at[i, core, rows]
        pending.append(remote(ref, ref, sem_fw_s.at[part, w], sem_fw_r.at[part, w], sibling))
        if part == 0:
            ref = out_packed.at[i, core]
            pending.append(remote(ref, ref, sem_fwp_s.at[w], sem_fwp_r.at[w], sibling))

    gather = {}
    for t in range(4):
        for part in range(4):
            gens = order_of(part)
            rows = pl.ds(part * PART, PART)
            held = span(gens[:t])
            if t > 0:
                for copy in gather[part, t - 1]:
                    copy.wait()
            gather[part, t] = []
            for w in held:
                i = chip_at(w)
                ref = out_codes.at[i, core, rows]
                got = w ^ gens[t]
                gather[part, t].append(
                    remote(ref, ref, sem_ag_s.at[part, got], sem_ag_r.at[part, got], peers[gens[t]])
                )
                if part == 0:
                    ref = out_packed.at[i, core]
                    gather[part, t].append(
                        remote(ref, ref, sem_agp_s.at[got], sem_agp_r.at[got], peers[gens[t]])
                    )
            for w in held[len(held) // 2 :] if t > 0 else held:
                to_sibling(part, w)
    for part in range(4):
        gens = order_of(part)
        for copy in gather[part, 3]:
            copy.wait()
        held = span(gens)
        for w in held[8:]:
            to_sibling(part, w)
    for copy in pending:
        copy.wait()


def pivot_block(block):
    n = BLK // 8
    eye = (
        lax.broadcasted_iota(jnp.int32, (BLK, BLK), 0) == lax.broadcasted_iota(jnp.int32, (BLK, BLK), 1)
    ).astype(F32)
    whole = jnp.concatenate([block, eye], axis=1)
    parts = [whole[8 * g : 8 * g + 8] for g in range(n)]
    sub = lax.broadcasted_iota(jnp.int32, (8, 128), 0)
    for k in range(0, BLK, 4):
        home, at = k // 8, k % 8
        cols = [
            [jnp.broadcast_to(parts[g][:, k + i : k + i + 1], (8, 128)) for g in range(home, n)] for i in range(4)
        ]
        rows = [parts[home][at + i : at + i + 1] for i in range(4)]
        steps = []
        roots = []
        for i in range(4):
            pivot = cols[i][0][at + i : at + i + 1]
            inverse = 1.0 / pivot
            roots.append(lax.rsqrt(pivot))
            steps.append(rows[i] * inverse)
            for j in range(i + 1, 4):
                rows[j] = rows[j] - cols[i][0][at + j : at + j + 1] * steps[i]
                factor = cols[j][0][at + i : at + i + 1] * inverse
                cols[j] = [c - b * factor for c, b in zip(cols[j], cols[i])]
        for g in range(home, n):
            new = parts[g]
            for i in range(4):
                new = new - cols[i][g - home] * steps[i]
            if g == home:
                new = jnp.where(sub > at + 3, new, parts[g])
                for i in range(4):
                    new = jnp.where(sub == at + i, rows[i] * roots[i], new)
            parts[g] = new
    return jnp.concatenate(parts, axis=0)[:, BLK:]


def ring_kernel(
    codes, packed, s_codes, s_packed, out_codes, out_packed, factor,
    first_in, second_in, third_in, third_out, sums, near_packed, third_packed_in, third_packed_out,
    high, low, gram_parts, gram_all, work,
    sem_a_s, sem_a_r, sem_p_s, sem_p_r, sem_c_s, sem_c_r, sem_cp_s, sem_cp_r,
    sem_g_s, sem_g_r, sem_gp_s, sem_gp_r, sem_y_s, sem_y_r, sem_w_s, sem_w_r,
):
    y = lax.axis_index("grp")
    me = lax.axis_index("col")
    near = (xor2(y, 1), xor2(y, 3))

    barrier = pltpu.get_barrier_semaphore()
    for d in range(1, 4):
        pl.semaphore_signal(barrier, inc=1, device_id={"grp": (y + d) % 4}, device_id_type=MESH)

    def greet(d, carry):
        pl.semaphore_signal(barrier, inc=1, device_id={"col": (me + d) % 32}, device_id_type=MESH)
        return carry

    lax.fori_loop(1, 32, greet, 0)
    pl.semaphore_wait(barrier, 34)

    def remote(src, dst, s, r, axis, peer):
        copy = pltpu.make_async_remote_copy(
            src_ref=src, dst_ref=dst, send_sem=s, recv_sem=r,
            device_id={axis: peer}, device_id_type=MESH,
        )
        copy.start()
        return copy

    def quarter(w):
        return pl.ds(pl.multiple_of(4 * xor2(y, w), 4), 4)

    gens = ((1, 3), (3, 1))
    ends = [pl.ds(h * HALF, HALF) for h in range(2)]
    line = {1: 0, 3: 1}

    scales = [remote(packed, near_packed.at[n], sem_p_s.at[n], sem_p_r.at[n], "grp", near[n]) for n in range(2)]
    first, second = [], []
    for h in range(2):
        g, g2 = gens[h]
        first.append(
            remote(codes.at[quarter(2), ends[h]], first_in.at[h], sem_a_s.at[h, 0], sem_a_r.at[h, 0], "grp", near[line[g]])
        )
    for h in range(2):
        g, g2 = gens[h]
        second.append(
            remote(codes.at[quarter(g), ends[h]], second_in.at[h], sem_a_s.at[h, 1], sem_a_r.at[h, 1], "grp", near[line[g]])
        )

    def widen(i, carry):
        for core in range(2):
            lanes = slice(core * 128, core * 128 + 128)
            a, b = split(decode(s_codes[i, core], unpack(s_packed[i, core], 0, K)))
            high[i, :K, lanes] = a
            low[i, :K, lanes] = b
        high[i, K:] = jnp.zeros((64, EDGE), BF16)
        low[i, K:] = jnp.zeros((64, EDGE), BF16)
        return carry

    lax.fori_loop(0, NB, widen, 0)
    block = me % 30
    rows = pl.ds(pl.multiple_of(32 * (block // 3), 32), 32)
    cols = pl.ds(pl.multiple_of(128 * (block % 3), 128), 128)

    def gram_step(i, acc):
        a, b = high[i, rows], low[i, rows]
        c, d = high[i, cols], low[i, cols]
        return acc + (nt(a, c) + (nt(a, d) + nt(b, c)))

    gram_parts[y] = lax.fori_loop(0, NB, gram_step, jnp.zeros((32, 128), F32))
    over_y = [
        remote(gram_parts.at[y], gram_parts.at[y], sem_y_s.at[d], sem_y_r.at[d], "grp", (y + d) % 4) for d in range(1, 4)
    ]

    for copy in scales:
        copy.wait()
    own_scale = unpack(packed[...], 0, K)

    def summed(h, w, takes, target):
        at = 4 * xor2(y, w)

        def body(j, peak):
            value = decode(codes[at + j, ends[h]], own_scale[h * HALF : h * HALF + HALF])
            for ref, scale in takes:
                value = value + decode(ref[h, j], scale)
            target[h, j] = value
            value = jnp.abs(value)
            return jnp.maximum(peak, jnp.maximum(value[:, :128], value[:, 128:]))

        return lax.fori_loop(0, 4, body, jnp.zeros((HALF, 128), F32))

    near_scale = []
    third = []
    for h in range(2):
        g, g2 = gens[h]
        near_scale.append(unpack(near_packed[line[g]], 20 * h, HALF))
        first[h].wait()
        scale, inverse = scale_of(summed(h, g2, [(first_in, near_scale[h])], sums))
        third_packed_out[h] = pack(scale)

        def code(j, carry):
            third_out[h, j] = encode(sums[h, j], inverse)
            return carry

        lax.fori_loop(0, 4, code, 0)
        third.append(
            (
                remote(third_packed_out.at[h], third_packed_in.at[h], sem_cp_s.at[h], sem_cp_r.at[h], "grp", near[line[g2]]),
                remote(third_out.at[h], third_in.at[h], sem_c_s.at[h], sem_c_r.at[h], "grp", near[line[g2]]),
            )
        )

    for copy in over_y:
        copy.wait()
    gram_all[me] = (gram_parts[0] + gram_parts[1]) + (gram_parts[2] + gram_parts[3])

    def spread(d):
        return pltpu.make_async_remote_copy(
            src_ref=gram_all.at[me], dst_ref=gram_all.at[me], send_sem=sem_w_s.at[d], recv_sem=sem_w_r.at[d],
            device_id={"col": (me + d) % 32}, device_id_type=MESH,
        )

    def spread_start(d, carry):
        spread(d).start()
        return carry

    def spread_wait(d, carry):
        spread(d).wait()
        return carry

    lax.fori_loop(1, 32, spread_start, 0)
    lax.fori_loop(1, 32, spread_wait, 0)

    for r in range(10):
        for c in range(3):
            work[32 * r : 32 * r + 32, 128 * c : 128 * c + 128] = gram_all[3 * r + c] * (1.0 / ROWS)
    work[:, 384:] = (
        lax.broadcasted_iota(jnp.int32, (K, 384), 0) == lax.broadcasted_iota(jnp.int32, (K, 384), 1)
    ).astype(F32)

    def eliminate(b):
        top, low_row = b * BLK, b * BLK + BLK
        inverse = pivot_block(work[top:low_row, top:low_row])
        panel = nn(inverse, work[top:low_row, :], precision=HIGHEST)
        work[top:low_row, :] = panel
        if low_row < K:
            left = panel[:, low_row:K]
            lane = low_row // 128 * 128
            work[low_row:, lane:384] -= tn(left, panel[:, lane:384], precision=HIGHEST)
            edge = 384 + (low_row + 127) // 128 * 128
            work[low_row:, 384:edge] -= tn(left, panel[:, 384:edge], precision=HIGHEST)

    gather, gather_packed = {}, {}

    def share_out(h):
        g, g2 = gens[h]
        second[h].wait()
        for copy in third[h]:
            copy.wait()
        third_scale = unpack(third_packed_in[h], 0, HALF)
        scale, inverse = scale_of(summed(h, 0, [(second_in, near_scale[h]), (third_in, third_scale)], sums))
        out_packed[y, h] = pack(scale)

        def code(j, carry):
            out_codes[4 * y + j, ends[h]] = encode(sums[h, j], inverse)
            return carry

        lax.fori_loop(0, 4, code, 0)
        send_quarter(h, 0, g2, 0)
        send_quarter(h, 0, g, 1)

    def send_quarter(h, w, g, n):
        ref = out_codes.at[quarter(w), ends[h]]
        gather[h, n] = remote(ref, ref, sem_g_s.at[h, n], sem_g_r.at[h, n], "grp", near[line[g]])
        ref = out_packed.at[xor2(y, w), h]
        gather_packed[h, n] = remote(ref, ref, sem_gp_s.at[h, n], sem_gp_r.at[h, n], "grp", near[line[g]])

    def pass_on(h):
        g, g2 = gens[h]
        gather[h, 0].wait()
        gather_packed[h, 0].wait()
        send_quarter(h, g2, g, 2)

    eliminate(0)
    for h in range(2):
        share_out(h)
    eliminate(1)
    eliminate(2)
    for h in range(2):
        pass_on(h)
    eliminate(3)
    eliminate(4)
    factor[...] = work[:, 384:]
    for h in range(2):
        for n in (1, 2):
            gather[h, n].wait()
            gather_packed[h, n].wait()


def final_kernel(codes, packed, share, factor, projected, basis, w_high, w_low):
    step = pl.program_id(0)

    @pl.when(step == 0)
    def _():
        w = factor[:, :K]
        a, b = split(w)
        w_high[...] = a
        w_low[...] = b
        basis[...] = nt(share[...].T, w, precision=HIGHEST)

    q = step // 2
    scale = jnp.concatenate([unpack(packed[q, 0], 0, HALF), unpack(packed[q, 1], 0, HALF)], axis=0)
    for j in range(2):
        a, b = split(decode(codes[j], scale).T)
        projected[EDGE * j : EDGE * j + EDGE, :] = nt(a, w_high[...]) + (nt(a, w_low[...]) + nt(b, w_high[...]))


def whole(shape):
    return pl.BlockSpec(shape, lambda *_: (0,) * len(shape))


def vmem(n):
    return [pl.BlockSpec(memory_space=pltpu.VMEM)] * n


def shape(dims, dtype):
    return jax.ShapeDtypeStruct(dims, dtype)


def local(tile_entries, slot_tile_row, slot_tile_column, tile_count, test_matrix):
    tiles_spec = pl.BlockSpec((GROUP, EDGE, EDGE), lambda i, *_: (i, 0, 0))
    scalars = (slot_tile_row, slot_tile_column, tile_count)
    params = pltpu.CompilerParams(vmem_limit_bytes=VMEM_LIMIT)

    codes, packed = pl.pallas_call(
        sample_kernel,
        grid_spec=pltpu.PrefetchScalarGridSpec(
            num_scalar_prefetch=3,
            grid=(SLOTS // GROUP,),
            in_specs=[tiles_spec, whole((NB * EDGE, K))],
            out_specs=[whole((NB, 2, K, 128)), whole((8, 128))],
            scratch_shapes=[pltpu.VMEM((NB, K, EDGE), BF16), pltpu.VMEM((NB + 1, K, EDGE), F32)],
        ),
        out_shape=[shape((NB, 2, K, 128), I16), shape((8, 128), F32)],
        compiler_params=params,
        name="sample",
    )(*scalars, tile_entries, test_matrix)

    dma = pltpu.SemaphoreType.DMA
    share, s_codes, s_packed = pl.pallas_call(
        plane_kernel,
        in_specs=vmem(2),
        out_specs=vmem(3),
        out_shape=[shape((K, 128), F32), shape((NB, 2, K, 128), I16), shape((NB, 2, 8, 128), F32)],
        scratch_shapes=[
            pltpu.VMEM((NB, K, 128), I16),
            pltpu.VMEM((8, 128), F32),
            pltpu.VMEM((NB, K, 128), F32),
        ]
        + [pltpu.VMEM((4, n, PART, 128), I16) for n in (8, 4, 2, 1)] * 2
        + [
            pltpu.VMEM((4, 4, 8, 128), F32),
            pltpu.VMEM((4, 4, 8, 128), F32),
            dma((4,)),
            dma((4, 4)), dma((4, 4)), dma((4, 4)), dma((4, 4)),
            dma((4, 16)), dma((4, 16)), dma((16,)), dma((16,)),
            dma((4, 16)), dma((4, 16)), dma((16,)), dma((16,)),
        ],
        compiler_params=pltpu.CompilerParams(
            vmem_limit_bytes=VMEM_LIMIT, collective_id=0, has_side_effects=True
        ),
        name="plane_sum",
    )(codes, packed)

    p_codes, p_packed = pl.pallas_call(
        project_kernel,
        grid_spec=pltpu.PrefetchScalarGridSpec(
            num_scalar_prefetch=3,
            grid=(SLOTS // GROUP,),
            in_specs=[tiles_spec, whole((NB, 2, K, 128)), whole((NB, 2, 8, 128))],
            out_specs=[whole((NB, K, EDGE)), whole((8, 128))],
            scratch_shapes=[pltpu.VMEM((NB, 2 * K, EDGE), BF16), pltpu.VMEM((NB + 1, K, EDGE), F32)],
        ),
        out_shape=[shape((NB, K, EDGE), I16), shape((8, 128), F32)],
        compiler_params=params,
        name="project",
    )(*scalars, tile_entries, s_codes, s_packed)

    block_in = pltpu.VMEM((2, 4, HALF, EDGE), I16)
    out_codes, out_packed, factor = pl.pallas_call(
        ring_kernel,
        in_specs=vmem(4),
        out_specs=vmem(3),
        out_shape=[shape((NB, K, EDGE), I16), shape((4, 2, 8, 128), F32), shape((K, 384), F32)],
        scratch_shapes=[
            block_in, block_in, block_in, block_in,
            pltpu.VMEM((2, 4, HALF, EDGE), F32),
            pltpu.VMEM((2, 8, 128), F32),
            pltpu.VMEM((2, 8, 128), F32),
            pltpu.VMEM((2, 8, 128), F32),
            pltpu.VMEM((NB, 384, EDGE), BF16),
            pltpu.VMEM((NB, 384, EDGE), BF16),
            pltpu.VMEM((4, 32, 128), F32),
            pltpu.VMEM((32, 32, 128), F32),
            pltpu.VMEM((K, 768), F32),
            dma((2, 2)), dma((2, 2)), dma((2,)), dma((2,)),
            dma((2,)), dma((2,)), dma((2,)), dma((2,)),
            dma((2, 3)), dma((2, 3)), dma((2, 3)), dma((2, 3)),
            dma((4,)), dma((4,)), dma((32,)), dma((32,)),
        ],
        compiler_params=pltpu.CompilerParams(
            vmem_limit_bytes=VMEM_LIMIT, collective_id=1, has_side_effects=True
        ),
        name="ring_sum",
    )(p_codes, p_packed, s_codes, s_packed)

    projected, basis = pl.pallas_call(
        final_kernel,
        grid=(8,),
        in_specs=[
            pl.BlockSpec((2, K, EDGE), lambda i: (i, 0, 0)),
            whole((4, 2, 8, 128)), whole((K, 128)), whole((K, 384)),
        ],
        out_specs=[pl.BlockSpec((2 * EDGE, K), lambda i: (i, 0)), whole((128, K))],
        out_shape=[shape((NB * EDGE, K), F32), shape((128, K), F32)],
        scratch_shapes=[pltpu.VMEM((K, K), BF16), pltpu.VMEM((K, K), BF16)],
        compiler_params=params,
        name="final",
    )(out_codes, out_packed, share, factor)
    return (basis, projected)


def solution(mesh):
    placed = (
        P(("grp", "col"), None, None),
        P(("grp", "col")),
        P(("grp", "col")),
        P(("grp", "col")),
        P("col", None),
    )
    return jax.shard_map(
        local,
        mesh=mesh,
        in_specs=placed,
        out_specs=(P(("grp", "col"), None), P("col", None)),
        check_vma=False,
    )
```

time: 667 us -> 180 us (0.27)
  waiting for transfers between devices: 388 us -> 0 us
  other arithmetic: 177 us -> 0 us
  Pallas kernels: 0 us -> 165 us
  matrix products: 38.7 us -> 0 us
  local copies, waits for them, and re-layouts: 44.2 us -> 12.5 us
  between operations: 16.6 us -> 1.3 us
    psum x2 -> x0, waiting for transfers between devices: 256 us -> none  [the longest x1 147 us: local(): gram = lax.psum(local_gram, ('grp', 'col')) / total_rows]
    pallas_call x0 -> x5, Pallas kernels: none -> 165 us  [the longest x1 64.9 us: local(): pl.pallas_call(ring_kernel, in_specs=vmem(4), out_specs=vmem(3), out_shap...]
    scatter-add x2 -> x0, other arithmetic: 93.1 us -> none  [padded_terms(): summed = empty.at[place_idx].add(products * live_mask[:, None, None])]
    reduce_scatter x1 -> x0, waiting for transfers between devices: 87.2 us -> none  [local(): lax.psum_scatter(partial_sample, 'col', scatter_dimension=0, tiled=True)]
    another operation x17 -> x0, other arithmetic: 80.2 us -> none  [the longest x10 50.5 us: orthonormal(): lower = jnp.linalg.cholesky(gram)]
    all_gather x1 -> x0, waiting for transfers between devices: 44.8 us -> none  [local(): lax.all_gather(basis.astype(jnp.bfloat16), 'col', axis=0, tiled=True)]
    dot_general x3 -> x0, matrix products: 34.1 us -> none  [the longest x2 31.8 us: padded_terms(): jnp.einsum(einsum_form, tile_entries, gathered, preferred_element_type=jn...]
    reshape x4 -> x0, local copies, waits for them, and re-layouts: 15.1 us -> none  [the longest x2 11.1 us: padded_terms(): return summed.reshape(out_blocks * edge_len, width)]
  transfers between devices with their start and end apart: 4 -> 0, of which waited for: 4 -> 0; matrix products, arithmetic and copies ran while one was open for 0% -> 0% of each run, Pallas kernels for 0% -> 0%
where the time goes in v1:
time: 180 us; the launch traced here: 179 us
  Pallas kernels  165 us (92%)
  local copies, waits for them, and re-layouts  12.5 us (7%)
    pallas_call x1, Pallas kernels, local(): pl.pallas_call(ring_kernel, in_specs=vmem(4), out_specs=vmem(3), out_shap...  64.9 us
    pallas_call x1, Pallas kernels, local(): pl.pallas_call(plane_kernel, in_specs=vmem(2), out_specs=vmem(3), out_sha...  52.9 us
    pallas_call x1, Pallas kernels, local(): pl.pallas_call(project_kernel, grid_spec=pltpu.PrefetchScalarGridSpec(num...  19.8 us
    pallas_call x1, Pallas kernels, local(): pl.pallas_call(sample_kernel, grid_spec=pltpu.PrefetchScalarGridSpec(num_...  15.4 us
    unnamed x3, local copies, waits for them, and re-layouts  12.5 us
    pallas_call x1, Pallas kernels, local(): pl.pallas_call(final_kernel, grid=(8,), in_specs=[pl.BlockSpec((2, K, EDG...  12.2 us

profile of v1, /device:TPU:0, one launch (start us, length us, event | category | flops | bytes accessed | tf_op | source)
XLA Modules:
  0.0 179.0 jit_solution(1454868841484897457)
XLA Ops:
  1.3 4.5 %copy.7.omega = bf16[4096,320]{1,0:T(8,128)(2,1)} copy(bf16[4096,320]{0,1:T(8,128)(2,1)} %param.9) | data formatting | bytes 5242880 | tf_op args[4]
  5.8 15.4 %sample.1 = (s16[16,2,320,128]{3,2,1,0:T(8,128)(2,1)}, f32[8,128]{1,0:T(8,128)}) custom-call(s32[72]{0:T(128)} %row_s.3, s32[72]{0:T(128)} %col_s.3, s32[1]{0:T(128)S(6)} %copy.10.count_s, bf16[72,256,256]{2,1,0:T(8,128)(2,1)} %tiles.3, bf16[4096,320]{1,0:T(8,128)(2,1)} %copy.7.omega), custom_call_target="tpu_custom_call" | custom-call | tf_op jit(solution)/shard_map/sample/pallas_call | solution.py:564
  21.3 52.9 %plane_sum.1 = (f32[320,128]{1,0:T(8,128)}, s16[16,2,320,128]{3,2,1,0:T(8,128)(2,1)}, f32[16,2,8,128]{3,2,1,0:T(8,128)}) custom-call(s16[16,2,320,128]{3,2,1,0:T(8,128)(2,1)} %get-tuple-element.14.codes, f32[8,128]{1,0:T(8,128)} %get-tuple-element.15.packed), custom_call_target="tpu_custom_call" | custom-call | tf_op jit(solution)/shard_map/plane_sum/pallas_call | solution.py:579
  74.1 19.8 %project.1 = (s16[16,320,256]{2,1,0:T(8,128)(2,1)}, f32[8,128]{1,0:T(8,128)}) custom-call(s32[72]{0:T(128)} %row_s.3, s32[72]{0:T(128)} %col_s.3, s32[1]{0:T(128)S(6)} %copy.10.count_s, bf16[72,256,256]{2,1,0:T(8,128)(2,1)} %tiles.3, s16[16,2,320,128]{3,2,1,0:T(8,128)(2,1)} %get-tuple-element.16.s_codes, f32[16,2,8,128]{3,2,1,0:T(8,128)} %get-tuple-element.17.s_packed), custom_call_target="tpu_custom_call" | custom-call | tf_op jit(solution)/shard_map/project/pallas_call | solution.py:604
  93.9 64.9 %ring_sum.1 = (s16[16,320,256]{2,1,0:T(8,128)(2,1)}, f32[4,2,8,128]{3,2,1,0:T(8,128)}, f32[320,384]{1,0:T(8,128)}) custom-call(s16[16,320,256]{2,1,0:T(8,128)(2,1)} %get-tuple-element.18.codes, f32[8,128]{1,0:T(8,128)} %get-tuple-element.19.packed, s16[16,2,320,128]{3,2,1,0:T(8,128)(2,1)} %get-tuple-element.16.s_codes, ...), custom_call_target="tpu_custom_call" | custom-call | tf_op jit(solution)/shard_map/ring_sum/pallas_call | solution.py:619
  158.8 12.2 %final.1 = (f32[4096,320]{1,0:T(8,128)}, f32[128,320]{1,0:T(8,128)}) custom-call(s16[16,320,256]{2,1,0:T(8,128)(2,1)} %get-tuple-element.20.codes, f32[4,2,8,128]{3,2,1,0:T(8,128)} %get-tuple-element.21.packed, f32[320,128]{1,0:T(8,128)} %get-tuple-element.22.share, f32[320,384]{1,0:T(8,128)} %get-tuple-element.23.factor), custom_call_target="tpu_custom_call" | custom-call | tf_op jit(solution)/shard_map/final/pallas_call | solution.py:646
  171.0 1.7 copy.8
  172.7 6.2 %copy.9 = f32[4096,320]{0,1:T(8,128)} copy(f32[4096,320]{1,0:T(8,128)} %get-tuple-element.27) | data formatting | bytes 10485760

commit v2 on v0

v2 whole, which is shorter than its diff:
```python
import functools

import jax
import jax.numpy as jnp
from jax import lax
from jax.experimental import pallas as pl
from jax.experimental.pallas import tpu as pltpu
from jax.sharding import PartitionSpec as P

MESH = pl.DeviceIdType.MESH
EDGE = 256
K = 320
HALF = 160
PART = 80
SLOTS = 72
GROUP = 8
GROUPS = SLOTS // GROUP
NB = 16
BLK = 64
ROWS = 16384
FCOLS = 4
FSTEPS = NB // FCOLS
F32 = jnp.float32
BF16 = jnp.bfloat16
I16 = jnp.int16
VMEM_LIMIT = 60 * 1024 * 1024
HIGHEST = lax.Precision.HIGHEST


def nn(a, b, **kw):
    return lax.dot_general(a, b, (((1,), (0,)), ((), ())), preferred_element_type=F32, **kw)


def nt(a, b, **kw):
    return lax.dot_general(a, b, (((1,), (1,)), ((), ())), preferred_element_type=F32, **kw)


def tn(a, b, **kw):
    return lax.dot_general(a, b, (((0,), (0,)), ((), ())), preferred_element_type=F32, **kw)


def scale_of(peak):
    top = jnp.maximum(jnp.max(peak, axis=1, keepdims=True), 1e-30)
    return top * (1.0 / 32767.0), 32767.0 / top


def encode(value, inverse):
    return jnp.round(value * inverse).astype(jnp.int32).astype(I16)


def decode(code, scale):
    return code.astype(jnp.int32).astype(F32) * scale


def pack(scale, first=0):
    lane = lax.broadcasted_iota(jnp.int32, (8, 128), 1)
    packed = jnp.zeros((8, 128), F32)
    for m in range(scale.shape[0] // 8):
        packed = jnp.where(lane == first + m, scale[8 * m : 8 * m + 8], packed)
    return packed


def unpack(packed, first, rows):
    return jnp.concatenate([packed[:, first + m : first + m + 1] for m in range(rows // 8)], axis=0)


def split(value):
    high = value.astype(BF16)
    return high, (value - high.astype(F32)).astype(BF16)


def sample_kernel(
    row_s, col_s, count_s, tiles_hbm, omega_hbm,
    codes, packed, order, order_row, start,
    tiles, omega, acc, fill, sems,
):
    load_omega = pltpu.make_async_copy(omega_hbm, omega, sems.at[GROUPS])
    load_omega.start()
    loads = []
    for n in range(GROUPS):
        part = pl.ds(n * GROUP, GROUP)
        loads.append(pltpu.make_async_copy(tiles_hbm.at[part], tiles.at[part], sems.at[n]))
        loads[-1].start()

    def clear(i, carry):
        acc[i] = jnp.zeros((K, EDGE), F32)
        return carry

    lax.fori_loop(0, NB, clear, 0)

    def bin_of(slot):
        return jnp.where(slot < count_s[0], col_s[slot], NB)

    for c in range(NB + 1):
        fill[c] = 0

    def count(slot, carry):
        c = bin_of(slot)
        fill[c] = fill[c] + 1
        return carry

    lax.fori_loop(0, SLOTS, count, 0)
    begin = jnp.int32(0)
    for c in range(NB + 1):
        start[c] = begin
        size = fill[c]
        fill[c] = begin
        begin = begin + size

    def put(slot, carry):
        c = bin_of(slot)
        at = fill[c]
        fill[c] = at + 1
        order[at] = slot
        order_row[at] = row_s[slot]
        return carry

    lax.fori_loop(0, SLOTS, put, 0)

    load_omega.wait()
    for n in range(GROUPS):
        loads[n].wait()
        for u in range(GROUP):
            slot = n * GROUP + u
            row = jnp.where(slot < count_s[0], row_s[slot], NB)
            left = omega[:, pl.ds(pl.multiple_of(col_s[slot] * EDGE, EDGE), EDGE)]
            acc[row] += nt(left, tiles[slot])

    def peak_step(i, peak):
        block = jnp.abs(acc[i])
        return jnp.maximum(peak, jnp.maximum(block[:, :128], block[:, 128:]))

    scale, inverse = scale_of(lax.fori_loop(0, NB, peak_step, jnp.zeros((K, 128), F32)))
    packed[...] = pack(scale)

    def code_step(i, carry):
        code = encode(acc[i], inverse)
        for ch in range(2):
            for core in range(2):
                codes[ch, i, core] = code[ch * HALF : ch * HALF + HALF, core * 128 : core * 128 + 128]
        return carry

    lax.fori_loop(0, NB, code_step, 0)


def xor2(a, b):
    return (a % 2 + b % 2) % 2 + 2 * ((a // 2 + b // 2) % 2)


def pivot_block(block):
    n = BLK // 8
    eye = (
        lax.broadcasted_iota(jnp.int32, (BLK, BLK), 0) == lax.broadcasted_iota(jnp.int32, (BLK, BLK), 1)
    ).astype(F32)
    whole = jnp.concatenate([block, eye], axis=1)
    parts = [whole[8 * g : 8 * g + 8] for g in range(n)]
    sub = lax.broadcasted_iota(jnp.int32, (8, 128), 0)
    for k in range(0, BLK, 4):
        home, at = k // 8, k % 8
        cols = [
            [jnp.broadcast_to(parts[g][:, k + i : k + i + 1], (8, 128)) for g in range(home, n)] for i in range(4)
        ]
        rows = [parts[home][at + i : at + i + 1] for i in range(4)]
        steps = []
        roots = []
        for i in range(4):
            pivot = cols[i][0][at + i : at + i + 1]
            inverse = 1.0 / pivot
            roots.append(lax.rsqrt(pivot))
            steps.append(rows[i] * inverse)
            for j in range(i + 1, 4):
                rows[j] = rows[j] - cols[i][0][at + j : at + j + 1] * steps[i]
                factor = cols[j][0][at + i : at + i + 1] * inverse
                cols[j] = [c - b * factor for c, b in zip(cols[j], cols[i])]
        for g in range(home, n):
            new = parts[g]
            for i in range(4):
                new = new - cols[i][g - home] * steps[i]
            if g == home:
                new = jnp.where(sub > at + 3, new, parts[g])
                for i in range(4):
                    new = jnp.where(sub == at + i, rows[i] * roots[i], new)
            parts[g] = new
    return jnp.concatenate(parts, axis=0)[:, BLK:]

def main_kernel(
    order, order_row, start, codes, packed, tiles_hbm,
    share, out_codes, out_packed, factor,
    pair_codes, pair_packed, total, sb, rb, sc, rc, sbp, rbp, scp, rcp, gat, gat_packed,
    s_split, tiles, prefix, p_codes, p_packed,
    first_in, second_in, third_in, third_out, sums, near_packed, third_packed_in, third_packed_out,
    gram_parts, gram_all, work,
    sem_t, sem_pair, sem_b, sem_c, sem_g1, sem_g2, sem_gp1, sem_gp2, sem_f, sem_fp,
    sem_a, sem_p, sem_3, sem_3p, sem_g, sem_gp, sem_y, sem_w,
):
    y = lax.axis_index("grp")
    me = lax.axis_index("col")
    chip, core = me // 2, me % 2
    x, z = chip // 4, chip % 4
    other = 1 - core
    sibling = {"col": chip * 2 + other}

    def along_x(d):
        return {"col": (xor2(x, d) * 4 + z) * 2 + core}

    def along_z(d):
        return {"col": (x * 4 + xor2(z, d)) * 2 + core}

    def along_y(d):
        return {"grp": xor2(y, d)}

    load_tiles = pltpu.make_async_copy(tiles_hbm, tiles, sem_t)
    load_tiles.start()

    barrier = pltpu.get_barrier_semaphore()
    greeted = [sibling] + [f(d) for f in (along_x, along_z, along_y) for d in (1, 2, 3)]
    for peer in greeted:
        pl.semaphore_signal(barrier, inc=1, device_id=peer, device_id_type=MESH)
    pl.semaphore_wait(barrier, len(greeted))

    def remote(src, dst, sems, peer):
        copy = pltpu.make_async_remote_copy(
            src_ref=src, dst_ref=dst, send_sem=sems.at[0], recv_sem=sems.at[1],
            device_id=peer, device_id_type=MESH,
        )
        copy.start()
        return copy

    pair = {
        ch: remote(codes.at[ch, :, other], pair_codes.at[ch], sem_pair.at[ch], sibling) for ch in range(2)
    }
    pair_scales = remote(packed, pair_packed, sem_pair.at[2], sibling)
    pair_scales.wait()

    def join(ch):
        pair[ch].wait()
        own_scale = unpack(packed[...], 20 * ch, HALF)
        pair_scale = unpack(pair_packed[...], 20 * ch, HALF)

        def body(w, carry):
            i = xor2(x, w // 4) * 4 + xor2(z, w % 4)
            total[ch, w] = decode(codes[ch, i, core], own_scale) + decode(pair_codes[ch, i], pair_scale)
            return carry

        lax.fori_loop(0, NB, body, 0)

    def block(p, a, b):
        return 4 * a + b if p == 0 else 4 * b + a

    outer = (along_x, along_z)
    inner = (along_z, along_x)
    part_rows = [slice(p * PART, p * PART + PART) for p in range(2)]
    part_at = [pl.ds(p * PART, PART) for p in range(2)]
    flying = {}

    def b_send(ch):
        for p in range(2):
            peak = jnp.zeros((PART, 128), F32)
            for d in range(1, 4):
                for e in range(4):
                    peak = jnp.maximum(peak, jnp.abs(total[ch, block(p, d, e), part_rows[p]]))
            scale, inverse = scale_of(peak)
            sbp[ch, p] = pack(scale)
            flying["b", ch, p] = []
            for d in range(1, 4):
                for e in range(4):
                    sb[ch, p, d - 1, e] = encode(total[ch, block(p, d, e), part_rows[p]], inverse)
                flying["b", ch, p] += [
                    remote(sb.at[ch, p, d - 1], rb.at[ch, p, d - 1], sem_b.at[ch, p, d - 1], outer[p](d)),
                    remote(sbp.at[ch, p], rbp.at[ch, p, d - 1], sem_b.at[ch, p, d + 2], outer[p](d)),
                ]

    def b_take(ch):
        for p in range(2):
            for copy in flying["b", ch, p]:
                copy.wait()
            scales = [unpack(rbp[ch, p, d], 0, PART) for d in range(3)]
            peak = jnp.zeros((PART, 128), F32)
            for e in range(4):
                at = block(p, 0, e)
                value = total[ch, at, part_rows[p]]
                for d in range(3):
                    value = value + decode(rb[ch, p, d, e], scales[d])
                total[ch, at, part_rows[p]] = value
                if e > 0:
                    peak = jnp.maximum(peak, jnp.abs(value))
            scale, inverse = scale_of(peak)
            scp[ch, p] = pack(scale)
            flying["c", ch, p] = []
            for e in range(1, 4):
                sc[ch, p, e - 1] = encode(total[ch, block(p, 0, e), part_rows[p]], inverse)
                flying["c", ch, p] += [
                    remote(sc.at[ch, p, e - 1], rc.at[ch, p, e - 1], sem_c.at[ch, p, e - 1], inner[p](e)),
                    remote(scp.at[ch, p], rcp.at[ch, p, e - 1], sem_c.at[ch, p, e + 2], inner[p](e)),
                ]

    def c_take(ch):
        for p in range(2):
            for copy in flying["c", ch, p]:
                copy.wait()
            value = total[ch, 0, part_rows[p]]
            for e in range(3):
                value = value + decode(rc[ch, p, e], unpack(rcp[ch, p, e], 0, PART))
            share[ch * HALF + p * PART : ch * HALF + p * PART + PART, :] = value
        mine = share[ch * HALF : ch * HALF + HALF, :]
        scale, inverse = scale_of(jnp.abs(mine))
        gat[ch, x, z, core] = encode(mine, inverse)
        gat_packed[ch, x, z, core] = pack(scale)
        flying["g1", ch] = []
        for d in range(1, 4):
            for p in range(2):
                ref = gat.at[ch, x, z, core, part_at[p]]
                flying["g1", ch].append(remote(ref, ref, sem_g1.at[ch, p, d], inner[p](d)))
            ref = gat_packed.at[ch, x, z, core]
            flying["g1", ch].append(remote(ref, ref, sem_gp1.at[ch, d], inner[0](d)))

    def g1_take(ch):
        for copy in flying["g1", ch]:
            copy.wait()
        flying["g2", ch] = []
        for d in range(1, 4):
            ref = gat.at[ch, x, :, core, part_at[0]]
            flying["g2", ch].append(remote(ref, ref, sem_g2.at[ch, 0, d], along_x(d)))
            ref = gat.at[ch, :, z, core, part_at[1]]
            flying["g2", ch].append(remote(ref, ref, sem_g2.at[ch, 1, d], along_z(d)))
            ref = gat_packed.at[ch, x, :, core]
            flying["g2", ch].append(remote(ref, ref, sem_gp2.at[ch, d], along_x(d)))

    def g2_take(ch):
        for copy in flying["g2", ch]:
            copy.wait()
        ref, packed_ref = gat.at[ch, :, :, core], gat_packed.at[ch, :, :, core]
        flying["f", ch] = [
            remote(ref, ref, sem_f.at[ch], sibling),
            remote(packed_ref, packed_ref, sem_fp.at[ch], sibling),
        ]

    def widen(ch):
        for copy in flying["f", ch]:
            copy.wait()

        def body(i, carry):
            for c in range(2):
                lanes = slice(c * 128, c * 128 + 128)
                scale = unpack(gat_packed[ch, i // 4, i % 4, c], 0, HALF)
                high, low = split(decode(gat[ch, i // 4, i % 4, c], scale))
                s_split[ch, i, :HALF, lanes] = high
                s_split[ch, i, HALF:, lanes] = low
            return carry

        lax.fori_loop(0, NB, body, 0)

    def project(ch):
        prefix[0] = jnp.zeros((HALF, EDGE), F32)

        def body(m, carry):
            for u in range(GROUP):
                n = m * GROUP + u
                both = nn(s_split[ch, order_row[n]], tiles[order[n]])
                prefix[n + 1] = prefix[n] + (both[:HALF] + both[HALF:])
            return carry

        lax.fori_loop(0, GROUPS, body, 0)

        def value_of(j):
            return prefix[start[j + 1]] - prefix[start[j]]

        def peak_step(j, peak):
            value = jnp.abs(value_of(j))
            return jnp.maximum(peak, jnp.maximum(value[:, :128], value[:, 128:]))

        scale, inverse = scale_of(lax.fori_loop(0, NB, peak_step, jnp.zeros((HALF, 128), F32)))
        p_packed[ch] = pack(scale)

        def code_step(j, carry):
            p_codes[ch, j] = encode(value_of(j), inverse)
            return carry

        lax.fori_loop(0, NB, code_step, 0)

    gens = ((1, 3), (3, 1))
    line = {1: 0, 3: 1}

    def quarter(w):
        return pl.ds(pl.multiple_of(4 * xor2(y, w), 4), 4)

    def y_send(ch):
        flying["p", ch] = [
            remote(p_packed.at[ch], near_packed.at[ch, n], sem_p.at[ch, n], along_y(g)) for n, g in enumerate((1, 3))
        ]
        for n, target in ((0, first_in), (1, second_in)):
            for h in range(2):
                g, g2 = gens[h]
                w = (2, g)[n]
                flying["a", ch, h, n] = remote(
                    p_codes.at[ch, quarter(w), part_at[h]], target.at[ch, h], sem_a.at[ch, h, n], along_y(g)
                )

    def summed(ch, h, w, takes):
        at = 4 * xor2(y, w)
        own_scale = unpack(p_packed[ch], 10 * h, PART)

        def body(j, peak):
            value = decode(p_codes[ch, at + j, part_rows[h]], own_scale)
            for ref, scale in takes:
                value = value + decode(ref[ch, h, j], scale)
            sums[j] = value
            value = jnp.abs(value)
            return jnp.maximum(peak, jnp.maximum(value[:, :128], value[:, 128:]))

        return lax.fori_loop(0, 4, body, jnp.zeros((PART, 128), F32))

    def near_scale(ch, h):
        return unpack(near_packed[ch, line[gens[h][0]]], 10 * h, PART)

    def y_third(ch):
        for copy in flying["p", ch]:
            copy.wait()
        for h in range(2):
            g, g2 = gens[h]
            flying["a", ch, h, 0].wait()
            scale, inverse = scale_of(summed(ch, h, g2, [(first_in, near_scale(ch, h))]))
            third_packed_out[ch, h] = pack(scale)

            def code(j, carry):
                third_out[ch, h, j] = encode(sums[j], inverse)
                return carry

            lax.fori_loop(0, 4, code, 0)
            flying["3", ch, h] = [
                remote(third_packed_out.at[ch, h], third_packed_in.at[ch, h], sem_3p.at[ch, h], along_y(g2)),
                remote(third_out.at[ch, h], third_in.at[ch, h], sem_3.at[ch, h], along_y(g2)),
            ]

    def send_quarter(ch, h, w, g, n):
        ref = out_codes.at[ch, quarter(w), part_at[h]]
        packed_ref = out_packed.at[xor2(y, w), ch, h]
        flying["q", ch, h, n] = [
            remote(ref, ref, sem_g.at[ch, h, n], along_y(g)),
            remote(packed_ref, packed_ref, sem_gp.at[ch, h, n], along_y(g)),
        ]

    def y_share(ch):
        for h in range(2):
            g, g2 = gens[h]
            flying["a", ch, h, 1].wait()
            for copy in flying["3", ch, h]:
                copy.wait()
            third_scale = unpack(third_packed_in[ch, h], 0, PART)
            scale, inverse = scale_of(
                summed(ch, h, 0, [(second_in, near_scale(ch, h)), (third_in, third_scale)])
            )
            out_packed[y, ch, h] = pack(scale)

            def code(j, carry):
                out_codes[ch, 4 * y + j, part_rows[h]] = encode(sums[j], inverse)
                return carry

            lax.fori_loop(0, 4, code, 0)
            send_quarter(ch, h, 0, g2, 0)
            send_quarter(ch, h, 0, g, 1)

    def y_pass(ch):
        for h in range(2):
            g, g2 = gens[h]
            for copy in flying["q", ch, h, 0]:
                copy.wait()
            send_quarter(ch, h, g2, g, 2)

    def y_end(ch):
        for h in range(2):
            for n in (1, 2):
                for copy in flying["q", ch, h, n]:
                    copy.wait()

    def gram_block():
        mine = me % 20
        tall, wide = mine // 2, mine % 2
        from_ch = tall // 5
        at = pl.multiple_of(32 * (tall % 5), 32)

        def body(m, acc):
            for u in range(4):
                i = 4 * m + u
                a = s_split[from_ch, i, pl.ds(at, 32)]
                b = s_split[from_ch, i, pl.ds(HALF + at, 32)]
                c = s_split[wide, i, :HALF]
                d = s_split[wide, i, HALF:]
                acc = acc + (nt(a, c) + (nt(a, d) + nt(b, c)))
            return acc

        gram_parts[y] = lax.fori_loop(0, NB // 4, body, jnp.zeros((32, HALF), F32))
        ref = gram_parts.at[y]
        flying["y"] = [remote(ref, ref, sem_y.at[d], along_y(d)) for d in range(1, 4)]

    def gram_z():
        for copy in flying["y"]:
            copy.wait()
        gram_all[x, z, core] = (gram_parts[0] + gram_parts[1]) + (gram_parts[2] + gram_parts[3])
        ref = gram_all.at[x, z, core]
        flying["w0"] = [remote(ref, ref, sem_w.at[d], along_z(d)) for d in range(1, 4)]

    def gram_x():
        for copy in flying["w0"]:
            copy.wait()
        ref = gram_all.at[x, :, core]
        flying["w1"] = [remote(ref, ref, sem_w.at[3 + d], along_x(d)) for d in range(1, 4)]

    def gram_pair():
        for copy in flying["w1"]:
            copy.wait()
        ref = gram_all.at[:, :, core]
        flying["w2"] = [remote(ref, ref, sem_w.at[0], sibling)]

    def gram_whole():
        for copy in flying["w2"]:
            copy.wait()
        for tall in range(10):
            for wide in range(2):
                n = 2 * tall + wide
                work[32 * tall : 32 * tall + 32, HALF * wide : HALF * wide + HALF] = gram_all[
                    n // 8, n // 2 % 4, n % 2
                ] * (1.0 / ROWS)
        work[:, K:384] = jnp.zeros((K, 384 - K), F32)
        work[:, 384:] = (
            lax.broadcasted_iota(jnp.int32, (K, 384), 0) == lax.broadcasted_iota(jnp.int32, (K, 384), 1)
        ).astype(F32)

    def eliminate(b):
        top, bottom = b * BLK, b * BLK + BLK
        inverse = pivot_block(work[top:bottom, top:bottom])
        panel = nn(inverse, work[top:bottom, :], precision=HIGHEST)
        work[top:bottom, :] = panel
        if bottom < K:
            left = panel[:, bottom:K]
            lane = bottom // 128 * 128
            work[bottom:, lane:384] -= tn(left, panel[:, lane:384], precision=HIGHEST)
            edge = 384 + (bottom + 127) // 128 * 128
            work[bottom:, 384:edge] -= tn(left, panel[:, 384:edge], precision=HIGHEST)

    def leave():
        factor[...] = work[:, 384:]

    schedule = [
        (join, 0), (b_send, 0), (join, 1), (b_take, 0), (c_take, 0), (b_send, 1), (g1_take, 0), (b_take, 1),
        (g2_take, 0), (c_take, 1), (widen, 0), (g1_take, 1), (load_tiles.wait,), (project, 0), (y_send, 0),
        (g2_take, 1), (widen, 1), (y_third, 0), (project, 1), (y_send, 1),
        (gram_block,), (y_third, 1), (y_share, 0), (gram_z,), (gram_x,), (gram_pair,), (y_share, 1), (gram_whole,),
        (y_pass, 0), (eliminate, 0), (eliminate, 1), (y_pass, 1), (eliminate, 2), (eliminate, 3), (eliminate, 4),
        (leave,), (y_end, 0), (y_end, 1),
    ]
    for stage, *of in schedule:
        stage(*of)


def final_kernel(codes, packed, share, factor, projected_t, basis_t, left, right):
    step = pl.program_id(0)

    @pl.when(step == 0)
    def _():
        w = factor[:, :K]
        high, low = split(w)
        left[:, :K] = high
        left[:, K : 2 * K] = high
        left[:, 2 * K :] = low
        basis_t[...] = nn(w, share[...], precision=HIGHEST)

    for j in range(FCOLS):
        q = (step * FCOLS + j) // 4
        for ch in range(2):
            scale = jnp.concatenate([unpack(packed[q, ch, 0], 0, PART), unpack(packed[q, ch, 1], 0, PART)], axis=0)
            high, low = split(decode(codes[ch, j], scale))
            at = ch * HALF
            right[at : at + HALF] = high
            right[K + at : K + at + HALF] = low
            right[2 * K + at : 2 * K + at + HALF] = high
        projected_t[:, EDGE * j : EDGE * j + EDGE] = nn(left[...], right[...])


def whole(dims):
    return pl.BlockSpec(dims, lambda *_: (0,) * len(dims))


def vmem(n):
    return [pl.BlockSpec(memory_space=pltpu.VMEM)] * n


def smem(n):
    return [pl.BlockSpec(memory_space=pltpu.SMEM)] * n


def shape(dims, dtype):
    return jax.ShapeDtypeStruct(dims, dtype)


def local(tile_entries, slot_tile_row, slot_tile_column, tile_count, test_matrix):
    anywhere = pl.BlockSpec(memory_space=pl.ANY)
    params = pltpu.CompilerParams(vmem_limit_bytes=VMEM_LIMIT)
    dma = pltpu.SemaphoreType.DMA
    I32 = jnp.int32
    V = pltpu.VMEM

    codes, packed, order, order_row, start = pl.pallas_call(
        sample_kernel,
        in_specs=smem(3) + [anywhere, anywhere],
        out_specs=vmem(2) + smem(3),
        out_shape=[
            shape((2, NB, 2, HALF, 128), I16), shape((8, 128), F32),
            shape((SLOTS,), I32), shape((SLOTS,), I32), shape((NB + 1,), I32),
        ],
        scratch_shapes=[
            V((SLOTS, EDGE, EDGE), BF16), V((K, NB * EDGE), BF16), V((NB + 1, K, EDGE), F32),
            pltpu.SMEM((NB + 1,), I32), dma((GROUPS + 1,)),
        ],
        compiler_params=params,
        name="sample",
    )(slot_tile_row, slot_tile_column, tile_count, tile_entries, test_matrix.T)

    quarters = V((2, 2, 4, PART, EDGE), I16)
    share, out_codes, out_packed, factor = pl.pallas_call(
        main_kernel,
        in_specs=smem(3) + vmem(2) + [anywhere],
        out_specs=vmem(4),
        out_shape=[
            shape((K, 128), F32), shape((2, NB, HALF, EDGE), I16), shape((4, 2, 2, 8, 128), F32), shape((K, 384), F32),
        ],
        scratch_shapes=[
            V((2, NB, HALF, 128), I16), V((8, 128), F32), V((2, NB, HALF, 128), F32),
            V((2, 2, 3, 4, PART, 128), I16), V((2, 2, 3, 4, PART, 128), I16),
            V((2, 2, 3, PART, 128), I16), V((2, 2, 3, PART, 128), I16),
            V((2, 2, 8, 128), F32), V((2, 2, 3, 8, 128), F32),
            V((2, 2, 8, 128), F32), V((2, 2, 3, 8, 128), F32),
            V((2, 4, 4, 2, HALF, 128), I16), V((2, 4, 4, 2, 8, 128), F32),
            V((2, NB, K, EDGE), BF16), V((SLOTS, EDGE, EDGE), BF16), V((SLOTS + 1, HALF, EDGE), F32),
            V((2, NB, HALF, EDGE), I16), V((2, 8, 128), F32),
            quarters, quarters, quarters, quarters, V((4, PART, EDGE), F32),
            V((2, 2, 8, 128), F32), V((2, 2, 8, 128), F32), V((2, 2, 8, 128), F32),
            V((4, 32, HALF), F32), V((4, 4, 2, 32, HALF), F32), V((K, 768), F32),
            dma, dma((3, 2)), dma((2, 2, 6, 2)), dma((2, 2, 6, 2)),
            dma((2, 2, 4, 2)), dma((2, 2, 4, 2)), dma((2, 4, 2)), dma((2, 4, 2)), dma((2, 2)), dma((2, 2)),
            dma((2, 2, 2, 2)), dma((2, 2, 2)), dma((2, 2, 2)), dma((2, 2, 2)),
            dma((2, 2, 3, 2)), dma((2, 2, 3, 2)), dma((4, 2)), dma((7, 2)),
        ],
        compiler_params=pltpu.CompilerParams(
            vmem_limit_bytes=VMEM_LIMIT, collective_id=0, has_side_effects=True
        ),
        name="plane_and_ring_sums",
    )(order, order_row, start, codes, packed, tile_entries)

    projected_t, basis_t = pl.pallas_call(
        final_kernel,
        grid=(FSTEPS,),
        in_specs=[
            pl.BlockSpec((2, FCOLS, HALF, EDGE), lambda i: (0, i, 0, 0)),
            whole((4, 2, 2, 8, 128)), whole((K, 128)), whole((K, 384)),
        ],
        out_specs=[pl.BlockSpec((K, FCOLS * EDGE), lambda i: (0, i)), whole((K, 128))],
        out_shape=[shape((K, NB * EDGE), F32), shape((K, 128), F32)],
        scratch_shapes=[V((K, 3 * K), BF16), V((3 * K, EDGE), BF16)],
        compiler_params=params,
        name="final",
    )(out_codes, out_packed, share, factor)
    return (basis_t.T, projected_t.T)


def solution(mesh):
    placed = (
        P(("grp", "col"), None, None),
        P(("grp", "col")),
        P(("grp", "col")),
        P(("grp", "col")),
        P("col", None),
    )
    return jax.shard_map(
        local,
        mesh=mesh,
        in_specs=placed,
        out_specs=(P(("grp", "col"), None), P("col", None)),
        check_vma=False,
    )
```

time: 667 us -> 125 us (0.19)
  waiting for transfers between devices: 388 us -> 0 us
  other arithmetic: 177 us -> 0 us
  Pallas kernels: 0 us -> 122 us
  local copies, waits for them, and re-layouts: 44.2 us -> 0 us
  matrix products: 38.7 us -> 0 us
  between operations: 16.6 us -> 1.29 us
    psum x2 -> x0, waiting for transfers between devices: 256 us -> none  [the longest x1 147 us: local(): gram = lax.psum(local_gram, ('grp', 'col')) / total_rows]
    pallas_call x0 -> x3, Pallas kernels: none -> 122 us  [the longest x1 103 us: local(): pl.pallas_call(main_kernel, in_specs=smem(3) + vmem(2) + [anywhere], out_...]
    scatter-add x2 -> x0, other arithmetic: 93.1 us -> none  [padded_terms(): summed = empty.at[place_idx].add(products * live_mask[:, None, None])]
    reduce_scatter x1 -> x0, waiting for transfers between devices: 87.2 us -> none  [local(): lax.psum_scatter(partial_sample, 'col', scatter_dimension=0, tiled=True)]
    another operation x17 -> x0, other arithmetic: 80.2 us -> none  [the longest x10 50.5 us: orthonormal(): lower = jnp.linalg.cholesky(gram)]
    all_gather x1 -> x0, waiting for transfers between devices: 44.8 us -> none  [local(): lax.all_gather(basis.astype(jnp.bfloat16), 'col', axis=0, tiled=True)]
    dot_general x3 -> x0, matrix products: 34.1 us -> none  [the longest x2 31.8 us: padded_terms(): jnp.einsum(einsum_form, tile_entries, gathered, preferred_element_type=jn...]
    reshape x4 -> x0, local copies, waits for them, and re-layouts: 15.1 us -> none  [the longest x2 11.1 us: padded_terms(): return summed.reshape(out_blocks * edge_len, width)]
  transfers between devices with their start and end apart: 4 -> 0, of which waited for: 4 -> 0; matrix products, arithmetic and copies ran while one was open for 0% -> 0% of each run, Pallas kernels for 0% -> 0%
where the time goes in v2:
time: 125 us; the launch traced here: 123 us
  Pallas kernels  122 us (98%)
  between operations  1.29 us (1%)
    pallas_call x1, Pallas kernels, local(): pl.pallas_call(main_kernel, in_specs=smem(3) + vmem(2) + [anywhere], out_...  103 us
    pallas_call x1, Pallas kernels, local(): pl.pallas_call(sample_kernel, in_specs=smem(3) + [anywhere, anywhere], ou...  11.2 us
    pallas_call x1, Pallas kernels, local(): pl.pallas_call(final_kernel, grid=(FSTEPS,), in_specs=[pl.BlockSpec((2, F...  7.89 us

profile of v2, /device:TPU:0, one launch (start us, length us, event | category | flops | bytes accessed | tf_op | source)
XLA Modules:
  0.0 123.3 jit_solution(3866536946286014180)
XLA Ops:
  1.3 11.2 %sample.1 = (s16[2,16,2,160,128]{4,3,2,1,0:T(8,128)(2,1)}, f32[8,128]{1,0:T(8,128)}, s32[72]{0:T(128)}, s32[72]{0:T(128)}, s32[17]{0:T(128)}) custom-call(s32[72]{0:T(128)} %row_s.1, s32[72]{0:T(128)} %col_s.1, s32[1]{0:T(128)S(6)} %copy.7.count_s, bf16[72,256,256]{2,1,0:T(8,128)(2,1)} %tiles_hbm.3, bf16[320,4096]{1,0:T(8,128)(2,1)} %bitcast.3), custom_call_target="tpu_custom_call" | custom-call | tf_op jit(solution)/shard_map/sample/pallas_call | solution.py:603
  12.5 102.9 %plane_and_ring_sums.1 = (f32[320,128]{1,0:T(8,128)}, s16[2,16,160,256]{3,2,1,0:T(8,128)(2,1)}, f32[4,2,2,8,128]{4,3,2,1,0:T(8,128)}, f32[320,384]{1,0:T(8,128)}) custom-call(s32[72]{0:T(128)} %get-tuple-element.13.order, s32[72]{0:T(128)} %get-tuple-element.14.order_row, s32[17]{0:T(128)} %get-tuple-element.15.start, ...), custom_call_target="tpu_custom_call" | custom-call | tf_op jit(solution)/shard_map/plane_and_ring_sums/pallas_call | solution.py:620
  115.4 7.9 %final.1 = (f32[320,4096]{1,0:T(8,128)}, f32[320,128]{1,0:T(8,128)}) custom-call(s16[2,16,160,256]{3,2,1,0:T(8,128)(2,1)} %get-tuple-element.18.codes, f32[4,2,2,8,128]{4,3,2,1,0:T(8,128)} %get-tuple-element.19.packed, f32[320,128]{1,0:T(8,128)} %get-tuple-element.20.share, f32[320,384]{1,0:T(8,128)} %get-tuple-element.21.factor), custom_call_target="tpu_custom_call" | custom-call | tf_op jit(solution)/shard_map/final/pallas_call | solution.py:650

commit v3 on v2

--- a/solution.py
+++ b/solution.py
@@ -13,12 +13,13 @@
 HALF = 160
 PART = 80
 SLOTS = 72
-GROUP = 8
+GROUP = 24
 GROUPS = SLOTS // GROUP
+RUN = 24
 NB = 16
 BLK = 64
 ROWS = 16384
-FCOLS = 4
+FCOLS = 8
 FSTEPS = NB // FCOLS
 F32 = jnp.float32
 BF16 = jnp.bfloat16
@@ -71,8 +72,8 @@
 
 def sample_kernel(
     row_s, col_s, count_s, tiles_hbm, omega_hbm,
-    codes, packed, order, order_row, start,
-    tiles, omega, acc, fill, sems,
+    codes, packed, plan,
+    tiles, omega, acc, fill, out, sems, sem_out,
 ):
     load_omega = pltpu.make_async_copy(omega_hbm, omega, sems.at[GROUPS])
     load_omega.start()
@@ -102,7 +103,7 @@
     lax.fori_loop(0, SLOTS, count, 0)
     begin = jnp.int32(0)
     for c in range(NB + 1):
-        start[c] = begin
+        plan[2 * SLOTS + c] = begin
         size = fill[c]
         fill[c] = begin
         begin = begin + size
@@ -111,8 +112,8 @@
         c = bin_of(slot)
         at = fill[c]
         fill[c] = at + 1
-        order[at] = slot
-        order_row[at] = row_s[slot]
+        plan[at] = slot
+        plan[SLOTS + at] = row_s[slot]
         return carry
 
     lax.fori_loop(0, SLOTS, put, 0)
@@ -137,10 +138,19 @@
         code = encode(acc[i], inverse)
         for ch in range(2):
             for core in range(2):
-                codes[ch, i, core] = code[ch * HALF : ch * HALF + HALF, core * 128 : core * 128 + 128]
+                out[i, ch, core] = code[ch * HALF : ch * HALF + HALF, core * 128 : core * 128 + 128]
+        pltpu.make_async_copy(out.at[i, 0], codes.at[0, i], sem_out.at[0, i]).start()
+        pltpu.make_async_copy(out.at[i, 1], codes.at[1, i], sem_out.at[1, i]).start()
         return carry
 
     lax.fori_loop(0, NB, code_step, 0)
+
+    def out_step(i, carry):
+        pltpu.make_async_copy(out.at[i, 0], codes.at[0, i], sem_out.at[0, i]).wait()
+        pltpu.make_async_copy(out.at[i, 1], codes.at[1, i], sem_out.at[1, i]).wait()
+        return carry
+
+    lax.fori_loop(0, NB, out_step, 0)
 
 
 def xor2(a, b):
@@ -184,14 +194,14 @@
     return jnp.concatenate(parts, axis=0)[:, BLK:]
 
 def main_kernel(
-    order, order_row, start, codes, packed, tiles_hbm,
-    share, out_codes, out_packed, factor,
-    pair_codes, pair_packed, total, sb, rb, sc, rc, sbp, rbp, scp, rcp, gat, gat_packed,
+    plan, codes, packed, tiles_hbm,
+    share, result, out_packed, factor,
+    out_codes, own_codes, pair_codes, pair_packed, total, sb, rb, sc, rc, sbp, rbp, scp, rcp, gat, gat_packed,
     s_split, tiles, prefix, p_codes, p_packed,
     first_in, second_in, third_in, third_out, sums, near_packed, third_packed_in, third_packed_out,
     gram_parts, gram_all, work,
-    sem_t, sem_pair, sem_b, sem_c, sem_g1, sem_g2, sem_gp1, sem_gp2, sem_f, sem_fp,
-    sem_a, sem_p, sem_3, sem_3p, sem_g, sem_gp, sem_y, sem_w,
+    sem_t, sem_own, sem_pair, sem_b, sem_c, sem_g1, sem_g2, sem_gp1, sem_gp2, sem_f, sem_fp,
+    sem_a, sem_p, sem_3, sem_3p, sem_g, sem_gp, sem_y, sem_w, sem_out,
 ):
     y = lax.axis_index("grp")
     me = lax.axis_index("col")
@@ -210,7 +220,6 @@
         return {"grp": xor2(y, d)}
 
     load_tiles = pltpu.make_async_copy(tiles_hbm, tiles, sem_t)
-    load_tiles.start()
 
     barrier = pltpu.get_barrier_semaphore()
     greeted = [sibling] + [f(d) for f in (along_x, along_z, along_y) for d in (1, 2, 3)]
@@ -229,17 +238,21 @@
     pair = {
         ch: remote(codes.at[ch, :, other], pair_codes.at[ch], sem_pair.at[ch], sibling) for ch in range(2)
     }
+    own = {ch: pltpu.make_async_copy(codes.at[ch, :, core], own_codes.at[ch], sem_own.at[ch]) for ch in range(2)}
+    for ch in range(2):
+        own[ch].start()
     pair_scales = remote(packed, pair_packed, sem_pair.at[2], sibling)
     pair_scales.wait()
 
     def join(ch):
+        own[ch].wait()
         pair[ch].wait()
         own_scale = unpack(packed[...], 20 * ch, HALF)
         pair_scale = unpack(pair_packed[...], 20 * ch, HALF)
 
         def body(w, carry):
             i = xor2(x, w // 4) * 4 + xor2(z, w % 4)
-            total[ch, w] = decode(codes[ch, i, core], own_scale) + decode(pair_codes[ch, i], pair_scale)
+            total[ch, w] = decode(own_codes[ch, i], own_scale) + decode(pair_codes[ch, i], pair_scale)
             return carry
 
         lax.fori_loop(0, NB, body, 0)
@@ -354,16 +367,16 @@
         prefix[0] = jnp.zeros((HALF, EDGE), F32)
 
         def body(m, carry):
-            for u in range(GROUP):
-                n = m * GROUP + u
-                both = nn(s_split[ch, order_row[n]], tiles[order[n]])
+            for u in range(RUN):
+                n = m * RUN + u
+                both = nn(s_split[ch, plan[SLOTS + n]], tiles[plan[n]])
                 prefix[n + 1] = prefix[n] + (both[:HALF] + both[HALF:])
             return carry
 
-        lax.fori_loop(0, GROUPS, body, 0)
+        lax.fori_loop(0, SLOTS // RUN, body, 0)
 
         def value_of(j):
-            return prefix[start[j + 1]] - prefix[start[j]]
+            return prefix[plan[2 * SLOTS + j + 1]] - prefix[plan[2 * SLOTS + j]]
 
         def peak_step(j, peak):
             value = jnp.abs(value_of(j))
@@ -384,17 +397,22 @@
     def quarter(w):
         return pl.ds(pl.multiple_of(4 * xor2(y, w), 4), 4)
 
-    def y_send(ch):
+    def y_start(ch, n):
+        for h in range(2):
+            g, g2 = gens[h]
+            w, target = ((2, first_in), (g, second_in))[n]
+            flying["a", ch, h, n] = remote(
+                p_codes.at[ch, quarter(w), part_at[h]], target.at[ch, h], sem_a.at[ch, h, n], along_y(g)
+            )
+
+    def y_first(ch):
         flying["p", ch] = [
             remote(p_packed.at[ch], near_packed.at[ch, n], sem_p.at[ch, n], along_y(g)) for n, g in enumerate((1, 3))
         ]
-        for n, target in ((0, first_in), (1, second_in)):
-            for h in range(2):
-                g, g2 = gens[h]
-                w = (2, g)[n]
-                flying["a", ch, h, n] = remote(
-                    p_codes.at[ch, quarter(w), part_at[h]], target.at[ch, h], sem_a.at[ch, h, n], along_y(g)
-                )
+        y_start(ch, 0)
+
+    def y_second(ch):
+        y_start(ch, 1)
 
     def summed(ch, h, w, takes):
         at = 4 * xor2(y, w)
@@ -439,6 +457,13 @@
             remote(ref, ref, sem_g.at[ch, h, n], along_y(g)),
             remote(packed_ref, packed_ref, sem_gp.at[ch, h, n], along_y(g)),
         ]
+
+    written = []
+
+    def write(ch, h, w):
+        at = (ch, quarter(w), part_at[h])
+        written.append(pltpu.make_async_copy(out_codes.at[at], result.at[at], sem_out.at[ch, h, w]))
+        written[-1].start()
 
     def y_share(ch):
         for h in range(2):
@@ -459,6 +484,7 @@
             lax.fori_loop(0, 4, code, 0)
             send_quarter(ch, h, 0, g2, 0)
             send_quarter(ch, h, 0, g, 1)
+            write(ch, h, 0)
 
     def y_pass(ch):
         for h in range(2):
@@ -466,12 +492,14 @@
             for copy in flying["q", ch, h, 0]:
                 copy.wait()
             send_quarter(ch, h, g2, g, 2)
+            write(ch, h, g2)
 
     def y_end(ch):
         for h in range(2):
-            for n in (1, 2):
+            for n, w in ((1, gens[h][0]), (2, 2)):
                 for copy in flying["q", ch, h, n]:
                     copy.wait()
+                write(ch, h, w)
 
     def gram_block():
         mine = me % 20
@@ -542,15 +570,17 @@
         factor[...] = work[:, 384:]
 
     schedule = [
-        (join, 0), (b_send, 0), (join, 1), (b_take, 0), (c_take, 0), (b_send, 1), (g1_take, 0), (b_take, 1),
-        (g2_take, 0), (c_take, 1), (widen, 0), (g1_take, 1), (load_tiles.wait,), (project, 0), (y_send, 0),
-        (g2_take, 1), (widen, 1), (y_third, 0), (project, 1), (y_send, 1),
-        (gram_block,), (y_third, 1), (y_share, 0), (gram_z,), (gram_x,), (gram_pair,), (y_share, 1), (gram_whole,),
+        (join, 0), (b_send, 0), (join, 1), (load_tiles.start,), (b_take, 0), (c_take, 0), (b_send, 1), (g1_take, 0), (b_take, 1),
+        (g2_take, 0), (c_take, 1), (widen, 0), (g1_take, 1), (load_tiles.wait,), (project, 0), (y_first, 0), (y_second, 0),
+        (g2_take, 1), (widen, 1), (project, 1), (y_first, 1), (y_third, 0), (gram_block,), (y_second, 1),
+        (y_third, 1), (y_share, 0), (gram_z,), (gram_x,), (gram_pair,), (y_share, 1), (gram_whole,),
         (y_pass, 0), (eliminate, 0), (eliminate, 1), (y_pass, 1), (eliminate, 2), (eliminate, 3), (eliminate, 4),
         (leave,), (y_end, 0), (y_end, 1),
     ]
     for stage, *of in schedule:
         stage(*of)
+    for copy in written:
+        copy.wait()
 
 
 def final_kernel(codes, packed, share, factor, projected_t, basis_t, left, right):
@@ -600,17 +630,17 @@
     I32 = jnp.int32
     V = pltpu.VMEM
 
-    codes, packed, order, order_row, start = pl.pallas_call(
+    codes, packed, plan = pl.pallas_call(
         sample_kernel,
         in_specs=smem(3) + [anywhere, anywhere],
-        out_specs=vmem(2) + smem(3),
+        out_specs=[anywhere] + vmem(1) + smem(1),
         out_shape=[
             shape((2, NB, 2, HALF, 128), I16), shape((8, 128), F32),
-            shape((SLOTS,), I32), shape((SLOTS,), I32), shape((NB + 1,), I32),
+            shape((2 * SLOTS + NB + 1,), I32),
         ],
         scratch_shapes=[
             V((SLOTS, EDGE, EDGE), BF16), V((K, NB * EDGE), BF16), V((NB + 1, K, EDGE), F32),
-            pltpu.SMEM((NB + 1,), I32), dma((GROUPS + 1,)),
+            pltpu.SMEM((NB + 1,), I32), V((NB, 2, 2, HALF, 128), I16), dma((GROUPS + 1,)), dma((2, NB)),
         ],
         compiler_params=params,
         name="sample",
@@ -619,13 +649,13 @@
     quarters = V((2, 2, 4, PART, EDGE), I16)
     share, out_codes, out_packed, factor = pl.pallas_call(
         main_kernel,
-        in_specs=smem(3) + vmem(2) + [anywhere],
-        out_specs=vmem(4),
+        in_specs=smem(1) + [anywhere] + vmem(1) + [anywhere],
+        out_specs=vmem(1) + [anywhere] + vmem(2),
         out_shape=[
             shape((K, 128), F32), shape((2, NB, HALF, EDGE), I16), shape((4, 2, 2, 8, 128), F32), shape((K, 384), F32),
         ],
         scratch_shapes=[
-            V((2, NB, HALF, 128), I16), V((8, 128), F32), V((2, NB, HALF, 128), F32),
+            V((2, NB, HALF, EDGE), I16), V((2, NB, HALF, 128), I16), V((2, NB, HALF, 128), I16), V((8, 128), F32), V((2, NB, HALF, 128), F32),
             V((2, 2, 3, 4, PART, 128), I16), V((2, 2, 3, 4, PART, 128), I16),
             V((2, 2, 3, PART, 128), I16), V((2, 2, 3, PART, 128), I16),
             V((2, 2, 8, 128), F32), V((2, 2, 3, 8, 128), F32),
@@ -636,16 +666,16 @@
             quarters, quarters, quarters, quarters, V((4, PART, EDGE), F32),
             V((2, 2, 8, 128), F32), V((2, 2, 8, 128), F32), V((2, 2, 8, 128), F32),
             V((4, 32, HALF), F32), V((4, 4, 2, 32, HALF), F32), V((K, 768), F32),
-            dma, dma((3, 2)), dma((2, 2, 6, 2)), dma((2, 2, 6, 2)),
+            dma, dma((2,)), dma((3, 2)), dma((2, 2, 6, 2)), dma((2, 2, 6, 2)),
             dma((2, 2, 4, 2)), dma((2, 2, 4, 2)), dma((2, 4, 2)), dma((2, 4, 2)), dma((2, 2)), dma((2, 2)),
             dma((2, 2, 2, 2)), dma((2, 2, 2)), dma((2, 2, 2)), dma((2, 2, 2)),
-            dma((2, 2, 3, 2)), dma((2, 2, 3, 2)), dma((4, 2)), dma((7, 2)),
+            dma((2, 2, 3, 2)), dma((2, 2, 3, 2)), dma((4, 2)), dma((7, 2)), dma((2, 2, 4)),
         ],
         compiler_params=pltpu.CompilerParams(
             vmem_limit_bytes=VMEM_LIMIT, collective_id=0, has_side_effects=True
         ),
         name="plane_and_ring_sums",
-    )(order, order_row, start, codes, packed, tile_entries)
+    )(plan, codes, packed, tile_entries)
 
     projected_t, basis_t = pl.pallas_call(
         final_kernel,

time: 125 us -> 120 us (0.960); the launches traced: 123 us -> 120 us
  Pallas kernels: 122 us -> 119 us
    pallas_call x1, Pallas kernels: 103 us -> 101 us  [local(): pl.pallas_call(main_kernel, in_specs=smem(1) + [anywhere] + vmem(1) + [an...]
where the time goes in v3:
time: 120 us
  Pallas kernels  119 us (99%)
  between operations  1.29 us (1%)
    pallas_call x1, Pallas kernels, local(): pl.pallas_call(main_kernel, in_specs=smem(1) + [anywhere] + vmem(1) + [an...  101 us
    pallas_call x1, Pallas kernels, local(): pl.pallas_call(sample_kernel, in_specs=smem(3) + [anywhere, anywhere], ou...  10.8 us
    pallas_call x1, Pallas kernels, local(): pl.pallas_call(final_kernel, grid=(FSTEPS,), in_specs=[pl.BlockSpec((2, F...  7.17 us

profile of v3, /device:TPU:0, one launch (start us, length us, event | category | flops | bytes accessed | tf_op | source)
XLA Modules:
  0.0 120.2 jit_solution(4812626170592464357)
XLA Ops:
  1.3 10.8 %sample.1 = (s16[2,16,2,160,128]{4,3,2,1,0:T(8,128)(2,1)}, f32[8,128]{1,0:T(8,128)}, s32[161]{0:T(256)}) custom-call(s32[72]{0:T(128)} %row_s.1, s32[72]{0:T(128)} %col_s.1, s32[1]{0:T(128)S(6)} %copy.7.count_s, bf16[72,256,256]{2,1,0:T(8,128)(2,1)} %tiles_hbm.3, bf16[320,4096]{1,0:T(8,128)(2,1)} %bitcast.3), custom_call_target="tpu_custom_call" | custom-call | tf_op jit(solution)/shard_map/sample/pallas_call | solution.py:633
  12.1 100.9 %plane_and_ring_sums.1 = (f32[320,128]{1,0:T(8,128)}, s16[2,16,160,256]{3,2,1,0:T(8,128)(2,1)}, f32[4,2,2,8,128]{4,3,2,1,0:T(8,128)}, f32[320,384]{1,0:T(8,128)}) custom-call(s32[161]{0:T(256)} %get-tuple-element.11.plan, s16[2,16,2,160,128]{4,3,2,1,0:T(8,128)(2,1)} %get-tuple-element.12.codes, f32[8,128]{1,0:T(8,128)} %get-tuple-element.13.packed, ...), custom_call_target="tpu_custom_call" | custom-call | tf_op jit(solution)/shard_map/plane_and_ring_sums/pallas_call | solution.py:650
  113.0 7.2 %final.1 = (f32[320,4096]{1,0:T(8,128)}, f32[320,128]{1,0:T(8,128)}) custom-call(s16[2,16,160,256]{3,2,1,0:T(8,128)(2,1)} %get-tuple-element.14.codes, f32[4,2,2,8,128]{4,3,2,1,0:T(8,128)} %get-tuple-element.15.packed, f32[320,128]{1,0:T(8,128)} %get-tuple-element.16.share, f32[320,384]{1,0:T(8,128)} %get-tuple-element.17.factor), custom_call_target="tpu_custom_call" | custom-call | tf_op jit(solution)/shard_map/final/pallas_call | solution.py:680

commit v4 on v3

--- a/solution.py
+++ b/solution.py
@@ -557,14 +557,15 @@
     def eliminate(b):
         top, bottom = b * BLK, b * BLK + BLK
         inverse = pivot_block(work[top:bottom, top:bottom])
-        panel = nn(inverse, work[top:bottom, :], precision=HIGHEST)
-        work[top:bottom, :] = panel
+        lane, edge = top // 128 * 128, 384 + (bottom + 127) // 128 * 128
+        panel = nn(inverse, work[top:bottom, lane:384], precision=HIGHEST)
+        known = nn(inverse, work[top:bottom, 384:edge], precision=HIGHEST)
+        work[top:bottom, 384:edge] = known
         if bottom < K:
-            left = panel[:, bottom:K]
-            lane = bottom // 128 * 128
-            work[bottom:, lane:384] -= tn(left, panel[:, lane:384], precision=HIGHEST)
-            edge = 384 + (bottom + 127) // 128 * 128
-            work[bottom:, 384:edge] -= tn(left, panel[:, 384:edge], precision=HIGHEST)
+            left = panel[:, bottom - lane : K - lane]
+            start = bottom // 128 * 128
+            work[bottom:, start:384] -= tn(left, panel[:, start - lane :], precision=HIGHEST)
+            work[bottom:, 384:edge] -= tn(left, known, precision=HIGHEST)
 
     def leave():
         factor[...] = work[:, 384:]
@@ -573,8 +574,8 @@
         (join, 0), (b_send, 0), (join, 1), (load_tiles.start,), (b_take, 0), (c_take, 0), (b_send, 1), (g1_take, 0), (b_take, 1),
         (g2_take, 0), (c_take, 1), (widen, 0), (g1_take, 1), (load_tiles.wait,), (project, 0), (y_first, 0), (y_second, 0),
         (g2_take, 1), (widen, 1), (project, 1), (y_first, 1), (y_third, 0), (gram_block,), (y_second, 1),
-        (y_third, 1), (y_share, 0), (gram_z,), (gram_x,), (gram_pair,), (y_share, 1), (gram_whole,),
-        (y_pass, 0), (eliminate, 0), (eliminate, 1), (y_pass, 1), (eliminate, 2), (eliminate, 3), (eliminate, 4),
+        (y_third, 1), (y_share, 0), (gram_z,), (gram_x,), (gram_pair,), (y_share, 1), (y_pass, 0), (gram_whole,),
+        (eliminate, 0), (eliminate, 1), (y_pass, 1), (eliminate, 2), (eliminate, 3), (eliminate, 4),
         (leave,), (y_end, 0), (y_end, 1),
     ]
     for stage, *of in schedule:

time: 120 us -> 120 us (level)
  no operation moved by 1% of the time
where the time goes in v4:
time: 120 us
  Pallas kernels  119 us (99%)
  between operations  1.29 us (1%)
    pallas_call x1, Pallas kernels, local(): pl.pallas_call(main_kernel, in_specs=smem(1) + [anywhere] + vmem(1) + [an...  101 us
    pallas_call x1, Pallas kernels, local(): pl.pallas_call(sample_kernel, in_specs=smem(3) + [anywhere, anywhere], ou...  10.9 us
    pallas_call x1, Pallas kernels, local(): pl.pallas_call(final_kernel, grid=(FSTEPS,), in_specs=[pl.BlockSpec((2, F...  7.18 us

profile of v4, /device:TPU:0, one launch (start us, length us, event | category | flops | bytes accessed | tf_op | source)
XLA Modules:
  0.0 120.0 jit_solution(1991503490580256310)
XLA Ops:
  1.3 10.9 %sample.1 = (s16[2,16,2,160,128]{4,3,2,1,0:T(8,128)(2,1)}, f32[8,128]{1,0:T(8,128)}, s32[161]{0:T(256)}) custom-call(s32[72]{0:T(128)} %row_s.1, s32[72]{0:T(128)} %col_s.1, s32[1]{0:T(128)S(6)} %copy.7.count_s, bf16[72,256,256]{2,1,0:T(8,128)(2,1)} %tiles_hbm.3, bf16[320,4096]{1,0:T(8,128)(2,1)} %bitcast.3), custom_call_target="tpu_custom_call" | custom-call | tf_op jit(solution)/shard_map/sample/pallas_call | solution.py:634
  12.1 100.7 %plane_and_ring_sums.1 = (f32[320,128]{1,0:T(8,128)}, s16[2,16,160,256]{3,2,1,0:T(8,128)(2,1)}, f32[4,2,2,8,128]{4,3,2,1,0:T(8,128)}, f32[320,384]{1,0:T(8,128)}) custom-call(s32[161]{0:T(256)} %get-tuple-element.11.plan, s16[2,16,2,160,128]{4,3,2,1,0:T(8,128)(2,1)} %get-tuple-element.12.codes, f32[8,128]{1,0:T(8,128)} %get-tuple-element.13.packed, ...), custom_call_target="tpu_custom_call" | custom-call | tf_op jit(solution)/shard_map/plane_and_ring_sums/pallas_call | solution.py:651
  112.8 7.2 %final.1 = (f32[320,4096]{1,0:T(8,128)}, f32[320,128]{1,0:T(8,128)}) custom-call(s16[2,16,160,256]{3,2,1,0:T(8,128)(2,1)} %get-tuple-element.14.codes, f32[4,2,2,8,128]{4,3,2,1,0:T(8,128)} %get-tuple-element.15.packed, f32[320,128]{1,0:T(8,128)} %get-tuple-element.16.share, f32[320,384]{1,0:T(8,128)} %get-tuple-element.17.factor), custom_call_target="tpu_custom_call" | custom-call | tf_op jit(solution)/shard_map/final/pallas_call | solution.py:681
